TPU v7x, 256 devices: a whole 4x4x8 slice. The times are simulated.
256 devices in a mesh: chan: 16 (over y, x_hi, core), filt: 16 (over x_lo, z).
Axes of the slice: x: 4 (x_hi: 2, x_lo: 2; x = x_hi * 2 + x_lo), y: 4, z: 8, core: 2. Of those that a mesh axis runs over, the one named last changes fastest.
Arguments:
- activations: bfloat16 [2592, 2048], P(None, ('chan', 'filt')), may hold values from -6 to 6
- act_tangent: bfloat16 [2592, 2048], P(None, ('chan', 'filt')), may hold values from -6 to 6
- kernel: bfloat16 [9, 2048, 2048], P(None, 'chan', 'filt'), may hold values from -0.046875 to 0.046875
- kernel_tangent: bfloat16 [9, 2048, 2048], P(None, 'chan', 'filt'), may hold values from -0.046875 to 0.046875
- slope: bfloat16 [2592, 2048], P('chan', 'filt'), may hold values from 0.19921875 to 1.09375
- curvature: bfloat16 [2592, 2048], P('chan', 'filt'), may hold values from 0.29882812 to 3
Outputs:
- input_cotangent: bfloat16 [2592, 2048], P('filt', 'chan')
- kernel_product: float32 [9, 2048, 2048], P(None, 'chan', 'filt')
All inputs are finite; a program needn't handle non-finite values.
Results may differ from a plain program's by a relative error of at most 0.0047.
Values may be sent and summed in bfloat16 or wider, within the bound.
A program may use at most 192 MiB of HBM per device.

v0:
```python
import jax
import jax.numpy as jnp
from jax import lax
from jax.sharding import PartitionSpec as P

HH = 12
WW = 12


def gather_turned(arrays, axis, dims):
    turned = [jnp.moveaxis(a, dim, 0) for a, dim in zip(arrays, dims)]
    widths = [t[0].size for t in turned]
    both = jnp.concatenate([t.reshape(-1, w) for t, w in zip(turned, widths)], axis=1)
    out = lax.all_gather(both, axis, axis=0, tiled=True)
    tiles = jnp.split(out, [sum(widths[:k]) for k in range(1, len(widths))], axis=1)
    return tuple(
        (
            jnp.moveaxis(b.reshape(-1, *t.shape[1:]), 0, dim)
            for b, t, dim in zip(tiles, turned, dims)
        )
    )


def split_up(x, dim, devices):
    before, after = (x.shape[:dim], x.shape[dim + 1 :])
    return jnp.moveaxis(x.reshape(*before, devices, -1, *after), dim, 0)


def summed_on_arrival(x, axis, dim):
    devices = lax.axis_size(axis)
    tiles = lax.all_to_all(split_up(x, dim, devices), axis, 0, 0, tiled=True)
    return jnp.sum(tiles, axis=0)


def copy_for_each(x, axis):
    devices = lax.axis_size(axis)
    return lax.all_to_all(jnp.broadcast_to(x[None], (devices, *x.shape)), axis, 0, 0, tiled=True)


def joined_along(tiles, dim):
    tiles = jnp.moveaxis(tiles, 0, dim)
    shape = tiles.shape
    return tiles.reshape(*shape[:dim], shape[dim] * shape[dim + 1], *shape[dim + 2 :])


def collect(x, axis, dim):
    tiles = copy_for_each(x, axis)
    return joined_along(tiles, dim)


def windows(flat, flip):
    width = flat.shape[-1]
    image = flat.reshape(-1, HH, WW, width)
    padded = jnp.pad(image, ((0, 0), (1, 1), (1, 1), (0, 0)))
    result = []
    for row_tap in range(3):
        for col_tap in range(3):
            top = 2 - row_tap if flip else row_tap
            left = 2 - col_tap if flip else col_tap
            result.append(padded[:, top : top + HH, left : left + WW, :].reshape(-1, width))
    return result


def weigh(slope, curvature, tangent):
    slope_f = slope.astype(jnp.float32)
    return (slope_f * slope_f * curvature.astype(jnp.float32) * tangent).astype(jnp.bfloat16)


def per_device(activations, act_tangent, kernel, kernel_tangent, slope, curvature):
    acts_block, tans_block = gather_turned((activations, act_tangent), "filt", (1, 1))
    acts = windows(acts_block, False)
    tans = windows(tans_block, False)
    pixel_count = acts_block.shape[0]
    partial_value = jnp.zeros((pixel_count, kernel.shape[2]), jnp.float32)
    for tap in range(9):
        partial_value = partial_value + jnp.dot(
            tans[tap], kernel[tap], preferred_element_type=jnp.float32
        )
        partial_value = partial_value + jnp.dot(
            acts[tap], kernel_tangent[tap], preferred_element_type=jnp.float32
        )
    share = summed_on_arrival(partial_value, "chan", 0)
    mine = weigh(slope, curvature, share)
    weighted = collect(mine, "chan", 0)
    backs = windows(weighted, True)
    cot_part = jnp.zeros((pixel_count, kernel.shape[1]), jnp.float32)
    grads = []
    for tap in range(9):
        cot_part = cot_part + lax.dot_general(
            backs[tap], kernel[tap], (((1,), (1,)), ((), ())), preferred_element_type=jnp.float32
        )
        grads.append(
            lax.dot_general(
                acts[tap], weighted, (((0,), (0,)), ((), ())), preferred_element_type=jnp.float32
            )
        )
    kernel_product = jnp.stack(grads) / jnp.sqrt(jnp.float32(pixel_count))
    cotangent = summed_on_arrival(cot_part, "filt", 0).astype(jnp.bfloat16)
    return (cotangent, kernel_product)


def solution(mesh):
    return jax.shard_map(
        per_device,
        mesh=mesh,
        in_specs=(
            P(None, ("chan", "filt")),
            P(None, ("chan", "filt")),
            P(None, "chan", "filt"),
            P(None, "chan", "filt"),
            P("chan", "filt"),
            P("chan", "filt"),
        ),
        out_specs=(P("filt", "chan"), P(None, "chan", "filt")),
        check_vma=False,
    )
```

profile of v0, /device:TPU:1, one launch (start us, length us, event | category | flops | bytes accessed | tf_op | source)
XLA Modules:
  0.0 271.1 jit_solution(4135889138371216857)
XLA Ops:
  7.2 1.5 pad_maximum_fusion
  8.8 65.7 %all-gather.2.cloned.1.call-done = bf16[128,5184]{1,0:T(8,128)(2,1)} async-done(((bf16[8,5184]{1,0:T(8,128)(2,1)}), bf16[128,5184]{1,0:T(8,128)(2,1)}) %all-gather.2.cloned.1.call-update) | async-done | bytes 1327120 | tf_op jit(solution)/shard_map/all_gather | solution.py:14
  74.4 1.6 slice_bitcast_fusion.1
  76.8 1.1 reshape.98
  77.9 6.2 %pad_slice_fusion.16 = (bf16[18,12,12,128]{3,2,1,0:T(8,128)(2,1)}, bf16[18,12,12,128]{3,2,1,0:T(8,128)(2,1)}, bf16[18,12,12,128]{3,2,1,0:T(8,128)(2,1)}, bf16[18...) fusion(bf16[18,12,12,128]{3,2,1,0:T(8,128)(2,1)} %reshape.98), kind=kLoop, calls=%fused_computation.59 | loop fusion | bytes 5971968 | tf_op jit(solution)/shard_map/slice | solution.py:60
  84.1 2.1 reshape.114
  86.1 2.0 reshape.102
  88.2 2.1 reshape.104
  90.2 2.0 reshape.106
  92.3 2.1 reshape.108
  94.3 2.1 reshape.110
  96.4 1.0 reshape.112
  97.4 1.0 reshape.99
  98.4 3.3 %pad_slice_fusion.8 = (bf16[18,12,12,128]{3,2,1,0:T(8,128)(2,1)}, bf16[18,12,12,128]{3,2,1,0:T(8,128)(2,1)}, bf16[18,12,12,128]{3,2,1,0:T(8,128)(2,1)S(1)}, bf16...) fusion(bf16[18,12,12,128]{3,2,1,0:T(8,128)(2,1)S(1)} %reshape.100), kind=kLoop, calls=%fused_computation.51 | loop fusion | bytes 5971968 | tf_op jit(solution)/shard_map/slice | solution.py:60
  101.7 1.3 reshape.115
  103.0 2.0 reshape.103
  105.0 1.0 reshape.105
  106.0 1.3 reshape.107
  107.5 1.6 reshape.111
  109.1 1.3 reshape.113
  110.4 2.1 reshape.101
  112.4 1.5 fusion.39
  114.3 0.7 copy-done.18
  115.4 0.8 copy-done.6
  116.5 0.8 copy-done.17
  117.6 0.8 copy-done.4
  118.7 0.8 copy-done.16
  120.1 1.0 copy-done.10
  121.1 0.7 convolution_add_fusion.17
  122.2 0.7 copy-done.15
  123.6 0.8 copy-done.14
  125.0 0.8 copy-done.13
  126.5 0.7 copy-done.12
  127.5 1.4 convolution_add_fusion.8
  129.0 1.4 reshape.116
  130.4 37.2 %all_to_all.15 = f32[16,162,128]{2,1,0:T(8,128)} all-to-all(f32[16,162,128]{2,1,0:T(8,128)S(1)} %reshape.116), channel_id=1, replica_groups=mesh['chan'=16,'filt'=16] {'chan'}, dimensions={0} | all-to-all | bytes 2654208 | tf_op jit(solution)/shard_map/all_to_all | solution.py:31
  167.6 1.4 reduce_sum.18
  169.2 17.2 %all_to_all.16 = bf16[16,162,128]{2,1,0:T(8,128)(2,1)S(1)} all-to-all(bf16[16,162,128]{2,1,0:T(8,128)(2,1)S(1)} %broadcast_in_dim.2), channel_id=1, replica_groups=mesh['chan'=16,'filt'=16] {'chan'}, dimensions={0} | all-to-all | bytes 1327104 | tf_op jit(solution)/shard_map/all_to_all | solution.py:37
  186.3 1.1 reshape_reshape.3
  187.5 6.4 %pad_slice_fusion = (bf16[18,12,12,128]{3,2,1,0:T(8,128)(2,1)}, bf16[18,12,12,128]{3,2,1,0:T(8,128)(2,1)}, bf16[18,12,12,128]{3,2,1,0:T(8,128)(2,1)}, bf16[18,12...) fusion(bf16[18,12,12,128]{3,2,1,0:T(8,128)(2,1)} %reshape_reshape.3), kind=kLoop, calls=%fused_computation.43 | loop fusion | bytes 5971968 | tf_op jit(solution)/shard_map/slice | solution.py:60
  193.9 2.1 reshape.125
  195.9 2.1 reshape.118
  198.0 2.0 reshape.119
  200.0 1.3 reshape.120
  201.3 2.1 reshape.122
  203.4 2.0 reshape.123
  205.4 2.0 reshape.124
  207.5 2.0 reshape.117
  209.5 1.5 fusion.37
  211.0 1.2 convolution_add_fusion.7
  212.2 1.1 convolution_add_fusion.6
  213.3 2.2 convolution_add_fusion.5
  215.7 1.8 convolution_add_fusion.4
  217.4 1.2 convolution_add_fusion.3
  218.6 1.2 convolution_add_fusion.2
  219.8 1.2 convolution_add_fusion.1
  221.0 2.2 convolution_add_fusion
  223.2 2.5 reshape.126
  225.7 4.5 %all-to-all-start.2 = ((f32[16,162,128]{2,1,0:T(8,128)}), f32[16,162,128]{2,1,0:T(8,128)}, u32[]{:S(2)}, u32[]{:S(2)}) async-start(f32[16,162,128]{2,1,0:T(8,128)} %reshape.126), calls=%async_computation.2 | async-start | bytes 2752512 | tf_op jit(solution)/shard_map/all_to_all | solution.py:31
  230.6 0.7 copy-done.7
  234.9 0.4 fusion.1
  235.3 0.9 broadcast_multiply_fusion
  236.2 26.0 %all-to-all-done.2 = f32[16,162,128]{2,1,0:T(8,128)} async-done(((f32[16,162,128]{2,1,0:T(8,128)}), f32[16,162,128]{2,1,0:T(8,128)}, u32[]{:S(2)}, u32[]{:S(2)}) %all-to-all-start.2) | async-done | bytes 1327136 | tf_op jit(solution)/shard_map/all_to_all | solution.py:31
  262.2 2.0 reduce_sum.19
  (79 shorter events, 10.1 us)
Async XLA Ops:
  7.2 67.3 %all-gather.2.cloned.1.call-start = ((), (), s32[]{:S(2)}) async-start(), calls=%async_computation.3 | async-start | bytes 1427456 | tf_op jit(solution)/shard_map/all_gather | solution.py:14
  107.3 12.5 %copy-start.2 = (bf16[2592,128]{1,0:T(8,128)(2,1)}, bf16[2592,128]{1,0:T(8,128)(2,1)S(1)}, u32[]{:S(2)}) copy-start(bf16[2592,128]{1,0:T(8,128)(2,1)S(1)} %reshape.107) | copy-start | bytes 1990660
  107.5 15.8 %copy-start = (bf16[2592,128]{1,0:T(8,128)(2,1)}, bf16[2592,128]{1,0:T(8,128)(2,1)S(1)}, u32[]{:S(2)}) copy-start(bf16[2592,128]{1,0:T(8,128)(2,1)S(1)} %reshape.109) | copy-start | bytes 1990660
  112.4 1.5 copy-start.8
  112.4 1.5 copy-start.26
  113.9 1.1 copy-start.18
  113.9 1.2 copy-start.25
  115.1 1.1 copy-start.6
  116.2 1.1 copy-start.17
  117.3 1.1 copy-start.4
  118.4 1.1 copy-start.16
  119.8 1.3 copy-start.10
  121.9 1.1 copy-start.15
  123.3 1.1 copy-start.14
  124.7 1.1 copy-start.13
  126.1 1.1 copy-start.12
  167.6 1.4 copy-start.27
  167.6 1.4 copy-start.28
  209.5 1.5 copy-start.24
  211.0 1.2 copy-start.23
  215.6 1.8 copy-start.22
  217.4 1.2 copy-start.21
  218.6 1.2 copy-start.20
  219.8 1.2 copy-start.19
  225.7 4.5 %copy-start.9 = (bf16[2592,128]{1,0:T(8,128)(2,1)S(1)}, bf16[2592,128]{1,0:T(8,128)(2,1)}, u32[]{:S(2)}) copy-start(bf16[2592,128]{1,0:T(8,128)(2,1)} %reshape.101) | copy-start | bytes 1990660
  225.7 36.5 %all-to-all-start.2 = ((f32[16,162,128]{2,1,0:T(8,128)}), f32[16,162,128]{2,1,0:T(8,128)}, u32[]{:S(2)}, u32[]{:S(2)}) async-start(f32[16,162,128]{2,1,0:T(8,128)} %reshape.126), calls=%async_computation.2 | async-start | bytes 2752512 | tf_op jit(solution)/shard_map/all_to_all | solution.py:31
  230.2 1.1 copy-start.7
  230.3 1.5 copy-start.5
  231.3 1.1 copy-start.3
  231.7 1.4 copy-start.11
  232.5 1.2 copy-start.1
Sparse Core Ops, SparseCore 0:
  10.4 64.0 all-gather.1
where the time goes:
time: 274 us; the launch traced here: 271 us
  waiting for transfers between devices  91.7 us (33%)
  local copies, waits for them, and re-layouts  74.6 us (27%)
  blocking collectives  54.4 us (20%)
  matrix products  25.3 us (9%)
  between operations  14.6 us (5%)
  other arithmetic  5.89 us (2%)
  starting transfers between devices  4.57 us (2%)
    all_gather x1, waiting for transfers between devices, gather_turned(): out = lax.all_gather(both, axis, axis=0, tiled=True)  65.7 us
    reshape x25, local copies, waits for them, and re-layouts, windows(): result.append(padded[:, top:top + HH, left:left + WW, :].reshape(-1, width))  40.7 us
    all_to_all x1, blocking collectives, summed_on_arrival(): tiles = lax.all_to_all(split_up(x, dim, devices), axis, 0, 0, tiled=True)  37.2 us
    all_to_all x1, waiting for transfers between devices, summed_on_arrival(): tiles = lax.all_to_all(split_up(x, dim, devices), axis, 0, 0, tiled=True)  26 us
    all_to_all x1, blocking collectives, copy_for_each(): lax.all_to_all(jnp.broadcast_to(x[None], (devices, *x.shape)), axis, 0, 0...  17.2 us
    slice x3, local copies, waits for them, and re-layouts, windows(): result.append(padded[:, top:top + HH, left:left + WW, :].reshape(-1, width))  15.9 us
    dot_general x9, matrix products, per_device(): lax.dot_general(backs[tap], kernel[tap], (((1,), (1,)), ((), ())), prefer...  13.3 us
    unnamed x58, local copies, waits for them, and re-layouts  9.35 us
  transfers between devices with their start and end apart: 2, of which 2 were waited for; matrix products, arithmetic and copies ran while one was open for 2% of the time, Pallas kernels for 0%

commit v1 on v0

v1 whole, which is shorter than its diff:
```python
import jax
import jax.numpy as jnp
import numpy as np
from jax import lax
from jax.experimental import pallas as pl
from jax.experimental.pallas import tpu as pltpu
from jax.sharding import PartitionSpec as P

HH = 12
WW = 12
IMAGE = HH * WW
PIXELS = 2592
LANES = 2688
CUT = 1152
SHARE = 162
ROWS = 176
PAD = 16
BLOCK = 384
TAPS = 9
BF = jnp.bfloat16
F32 = jnp.float32


def row_masks():
    r = np.arange(IMAGE + ROWS)
    i, j = (r // WW) % HH, r % WW
    m = np.stack([i >= 1, i <= HH - 2, j >= 1, j <= WW - 2]).astype(np.float32)
    return np.ascontiguousarray(np.broadcast_to(m[:, :, None], (*m.shape, 128)))


def lane_masks():
    p = np.arange(LANES)
    i, j = (p // WW) % HH, p % WW
    m = np.zeros((16, LANES), np.float32)
    for a in range(3):
        for e in range(3):
            si, sj = i + a - 1, j + e - 1
            m[3 * a + e] = (si >= 0) & (si < HH) & (sj >= 0) & (sj < WW) & (p < PIXELS)
    return m


def body(
    acts_ref, tans_ref, w_ref, v_ref, slope_ref, curv_ref, rmask, lmask,
    cot_ref, kp_ref,
    gath, wcat, taps, xts, w32, w16, sib_out, sib_in, red_out, red_in, own,
    wgt, cx_out, cx_in, cz_out, cz_in,
    a_ss, a_rs, p_rs, s_ss, s_rs, b_ss, b_rs, w_ss, w_rs, x_ss, x_rs, d_ss, d_rs,
):
    chan = lax.axis_index("chan")
    filt = lax.axis_index("filt")
    core = lax.rem(chan, 2)
    chip = lax.div(chan, 2)
    half = lax.div(filt, 8)
    z = lax.rem(filt, 8)
    other = 1 - core
    sibling = {"chan": 2 * chip + other, "filt": filt}
    across = {"chan": chan, "filt": (1 - half) * 8 + z}

    def at_z(d):
        return lax.rem(z + d + 8, 8)

    def z_dev(d):
        return {"chan": chan, "filt": half * 8 + at_z(d)}

    def chip_at(d):
        return lax.rem(chip + d + 8, 8)

    def chip_dev(d):
        return {"chan": 2 * chip_at(d) + core, "filt": filt}

    def remote(src, dst, ss, rs, dev):
        return pltpu.make_async_remote_copy(
            src_ref=src, dst_ref=dst, send_sem=ss, recv_sem=rs,
            device_id=dev, device_id_type=pl.DeviceIdType.MESH,
        )

    barrier = pltpu.get_barrier_semaphore()
    peers = [sibling, across]
    peers += [z_dev(d) for d in range(1, 8)] + [chip_dev(d) for d in range(1, 8)]
    for dev in peers:
        pl.semaphore_signal(barrier, inc=1, device_id=dev, device_id_type=pl.DeviceIdType.MESH)

    both = jnp.concatenate([acts_ref[...].astype(F32), tans_ref[...].astype(F32)], axis=0)
    both = jnp.concatenate([both, jnp.zeros((16, LANES - PIXELS), F32)], axis=1)
    gath[filt] = both.astype(BF)
    pl.semaphore_wait(barrier, len(peers))

    mine = half * 8
    theirs = (1 - half) * 8
    sent = []

    def send_full(slot, dev):
        n = len(sent)
        c = remote(gath.at[slot], gath.at[slot], a_ss.at[n], a_rs.at[slot], dev)
        c.start()
        sent.append(c)

    def low(slot):
        return gath.at[slot, :, pl.ds(0, CUT)]

    def high(slot):
        return gath.at[slot, :, pl.ds(CUT, LANES - CUT)]

    def send_low(slot, dev):
        n = len(sent)
        c = remote(low(slot), low(slot), a_ss.at[n], a_rs.at[slot], dev)
        c.start()
        sent.append(c)

    def send_high(slot, dev):
        n = len(sent)
        c = remote(high(slot), high(slot), a_ss.at[n], p_rs.at[slot], dev)
        c.start()
        sent.append(c)

    def got_full(slot):
        remote(gath.at[slot], gath.at[slot], a_ss.at[0], a_rs.at[slot], across).wait_recv()

    def got_low(slot):
        remote(low(slot), low(slot), a_ss.at[0], a_rs.at[slot], across).wait_recv()

    def got_high(slot):
        remote(high(slot), high(slot), a_ss.at[0], p_rs.at[slot], across).wait_recv()

    right, left = z_dev(1), z_dev(-1)
    send_full(filt, right)
    send_full(filt, left)
    send_full(filt, across)

    for k in range(TAPS):
        vk = v_ref[k].astype(F32).reshape(16, 1, 8, 128)
        wk = w_ref[k].astype(F32).reshape(16, 1, 8, 128)
        wcat[:, 128 * k:128 * k + 128] = (
            jnp.concatenate([vk, wk], axis=1).reshape(256, 128).astype(BF)
        )
        taps[k, 0:PAD, :] = jnp.zeros((PAD, 128), F32)

    for h in range(1, 6):
        if h <= 4:
            slot = mine + at_z(-h)
            got_full(slot)
            if h < 4:
                send_full(slot, right)
            send_high(slot, across)
        if h <= 3:
            slot = mine + at_z(h)
            got_full(slot)
            if h < 3:
                send_full(slot, left)
            send_high(slot, across)
        if h == 1:
            slot = theirs + z
            got_full(slot)
            send_low(slot, right)
            send_low(slot, left)
        else:
            slot = theirs + at_z(-(h - 1))
            got_low(slot)
            if h - 1 < 4:
                send_low(slot, right)
            if h - 1 <= 3:
                slot = theirs + at_z(h - 1)
                got_low(slot)
                if h - 1 < 3:
                    send_low(slot, left)
    for d in range(1, 8):
        got_high(theirs + at_z(d))

    def forward(t, _):
        lanes = pl.ds(pl.multiple_of(t * BLOCK, 128), BLOCK)
        rows = pl.ds(pl.multiple_of(PAD + t * BLOCK, 16), BLOCK)
        x = gath[:, :, lanes].reshape(256, BLOCK).T
        for k in range(0, TAPS, 2):
            width = min(2, TAPS - k)
            res = jnp.dot(x, wcat[:, 128 * k:128 * (k + width)], preferred_element_type=F32)
            for q in range(width):
                taps[k + q, rows, :] = res[:, 128 * q:128 * q + 128]
        return 0

    lax.fori_loop(0, LANES // BLOCK, forward, 0)

    def combined(c, flip, put):
        start = c * SHARE
        within = lax.rem(start, IMAGE)
        step = ROWS // 2
        for s in range(0, ROWS, step):
            m = [rmask[n, pl.ds(within + s, step), :] for n in range(4)]
            acc = None
            for a in range(3):
                part = None
                for e in range(3):
                    k = 3 * a + e
                    off = WW * (a - 1) + e - 1
                    val = taps[8 - k if flip else k, pl.ds(PAD + start + s + off, step), :]
                    if e == 0:
                        val = val * m[2]
                    if e == 2:
                        val = val * m[3]
                    part = val if part is None else part + val
                if a == 0:
                    part = part * m[0]
                if a == 2:
                    part = part * m[1]
                acc = part if acc is None else acc + part
            put(s, step, acc)

    def sib_copy(d):
        return remote(sib_out.at[d], sib_in.at[d], s_ss.at[d], s_rs.at[d], sibling)

    def to_sibling(j, _):
        d = chip_at(j + 1)

        def put(s, n, acc):
            sib_out[d, s:s + n, :] = acc

        combined(2 * d + other, False, put)
        sib_copy(d).start()
        return 0

    lax.fori_loop(0, 8, to_sibling, 0)

    def red_copy(j):
        d = chip_at(j)
        return remote(red_out.at[j], red_in.at[j], b_ss.at[j], b_rs.at[j], chip_dev(j))

    def to_chip(j, _):
        d = chip_at(j)
        sib_copy(d).wait_recv()

        def put(s, n, acc):
            red_out[j, s:s + n, :] = (acc + sib_in[d, s:s + n, :]).astype(BF)

        combined(2 * d + core, False, put)
        red_copy(j).start()
        return 0

    lax.fori_loop(1, 8, to_chip, 0)
    sib_copy(chip).wait_recv()

    def put_own(s, n, acc):
        own[s:s + n, :] = acc + sib_in[chip, s:s + n, :]

    combined(2 * chip + core, False, put_own)

    def shift(t, _):
        g = gath[pl.ds(2 * t, 2)].astype(F32)
        x = g[:, 0:8, :].reshape(16, LANES)
        rows = pl.ds(pl.multiple_of(16 * t, 16), 16)
        for e in range(3):
            xe = x if e == 1 else pltpu.roll(x, (1 - e) % LANES, 1)
            for a in range(3):
                k = 3 * a + e
                xk = xe if a == 1 else pltpu.roll(xe, (WW * (1 - a)) % LANES, 1)
                xts[k, rows, :] = (xk * lmask[k:k + 1, :]).astype(BF)
        return 0

    lax.fori_loop(0, 8, shift, 0)

    def add_in(j, _):
        red_copy(j).wait_recv()
        own[...] += red_in[j].astype(F32)
        return 0

    lax.fori_loop(1, 8, add_in, 0)
    slope = slope_ref[...].astype(F32)
    weighted = slope * slope * curv_ref[...].astype(F32) * own[0:SHARE, :]
    weighted = jnp.concatenate([weighted, jnp.zeros((ROWS - SHARE, 128), F32)], axis=0)
    wgt[chan] = weighted.astype(BF)

    def wgt_copy(slot, n, dev):
        return remote(wgt.at[slot], wgt.at[slot], w_ss.at[n], w_rs.at[slot], dev)

    def spread(j, _):
        wgt_copy(chan, j, chip_dev(j)).start()
        return 0

    lax.fori_loop(1, 8, spread, 0)
    wgt_copy(chan, 0, sibling).start()

    def pass_on(j, _):
        slot = 2 * chip_at(-j) + core
        wgt_copy(slot, 0, sibling).wait_recv()
        wgt_copy(slot, 7 + j, sibling).start()
        return 0

    lax.fori_loop(1, 8, pass_on, 0)

    def from_sibling(j, _):
        wgt_copy(2 * chip_at(-j) + other, 0, sibling).wait_recv()
        return 0

    lax.fori_loop(0, 8, from_sibling, 0)

    def compact(c, _):
        w32[pl.ds(c * SHARE, 168), :] = wgt[c, 0:168, :].astype(F32)
        return 0

    lax.fori_loop(0, 16, compact, 0)
    w32[PIXELS:LANES, :] = jnp.zeros((LANES - PIXELS, 128), F32)

    def backward(t, _):
        rows = pl.ds(pl.multiple_of(t * BLOCK, 16), BLOCK)
        spot = pl.ds(pl.multiple_of(PAD + t * BLOCK, 16), BLOCK)
        w = w32[rows, :].astype(BF)
        w16[rows, :] = w
        for k in range(0, TAPS, 2):
            width = min(2, TAPS - k)
            kern = w_ref[k:k + width].reshape(128 * width, 128)
            res = lax.dot_general(w, kern, (((1,), (1,)), ((), ())), preferred_element_type=F32)
            for q in range(width):
                taps[k + q, spot, :] = res[:, 128 * q:128 * q + 128]
        return 0

    lax.fori_loop(0, LANES // BLOCK, backward, 0)

    def cx_copy(j):
        return remote(cx_out.at[j], cx_in.at[j], x_ss.at[j], x_rs.at[j], across)

    def cz_copy(j):
        return remote(cz_out.at[j], cz_in.at[j], d_ss.at[j], d_rs.at[j], z_dev(j))

    def to_across(j, _):
        j = lax.rem(j + 1, 8)

        def put(s, n, acc):
            cx_out[j, s:s + n, :] = acc.astype(BF)

        combined(theirs + at_z(j), True, put)
        cx_copy(j).start()
        return 0

    lax.fori_loop(0, 8, to_across, 0)

    def to_z(j, _):
        cx_copy(j).wait_recv()

        def put(s, n, acc):
            cz_out[j, s:s + n, :] = (acc + cx_in[j, s:s + n, :].astype(F32)).astype(BF)

        combined(mine + at_z(j), True, put)
        cz_copy(j).start()
        return 0

    lax.fori_loop(1, 8, to_z, 0)
    cx_copy(0).wait_recv()

    def put_last(s, n, acc):
        own[s:s + n, :] = acc + cx_in[0, s:s + n, :].astype(F32)

    combined(mine + z, True, put_last)

    scale = F32(1.0) / jnp.sqrt(F32(PIXELS))

    def product(k, _):
        res = jnp.dot(xts[k], w16[...], preferred_element_type=F32)
        kp_ref[k] = res * scale
        return 0

    lax.fori_loop(0, TAPS, product, 0)

    def add_z(j, _):
        cz_copy(j).wait_recv()
        own[...] += cz_in[j].astype(F32)
        return 0

    lax.fori_loop(1, 8, add_z, 0)
    cot_ref[...] = own[0:SHARE, :].astype(BF)

    for c in sent:
        c.wait_send()

    def drain(j, _):
        sib_copy(j).wait_send()
        cx_copy(j).wait_send()
        wgt_copy(chan, j, sibling).wait_send()
        return 0

    lax.fori_loop(0, 8, drain, 0)

    def drain_far(j, _):
        red_copy(j).wait_send()
        cz_copy(j).wait_send()
        wgt_copy(chan, 7 + j, sibling).wait_send()
        return 0

    lax.fori_loop(1, 8, drain_far, 0)


def per_device(activations, act_tangent, kernel, kernel_tangent, slope, curvature):
    vm = pl.BlockSpec(memory_space=pltpu.VMEM)
    dma = pltpu.SemaphoreType.DMA
    share = (8, ROWS, 128)
    return pl.pallas_call(
        body,
        out_shape=(
            jax.ShapeDtypeStruct((SHARE, 128), BF),
            jax.ShapeDtypeStruct((TAPS, 128, 128), F32),
        ),
        in_specs=[vm] * 8,
        out_specs=(vm, vm),
        scratch_shapes=[
            pltpu.VMEM((16, 16, LANES), BF),
            pltpu.VMEM((256, TAPS * 128), BF),
            pltpu.VMEM((TAPS, PAD + LANES, 128), F32),
            pltpu.VMEM((TAPS, 128, LANES), BF),
            pltpu.VMEM((PAD + LANES, 128), F32),
            pltpu.VMEM((LANES, 128), BF),
            pltpu.VMEM(share, F32),
            pltpu.VMEM(share, F32),
            pltpu.VMEM(share, BF),
            pltpu.VMEM(share, BF),
            pltpu.VMEM((ROWS, 128), F32),
            pltpu.VMEM((16, ROWS, 128), BF),
            pltpu.VMEM(share, BF),
            pltpu.VMEM(share, BF),
            pltpu.VMEM(share, BF),
            pltpu.VMEM(share, BF),
            dma((24,)), dma((16,)), dma((16,)),
            dma((8,)), dma((8,)), dma((8,)), dma((8,)),
            dma((16,)), dma((16,)), dma((8,)), dma((8,)), dma((8,)), dma((8,)),
        ],
        compiler_params=pltpu.CompilerParams(
            collective_id=0, has_side_effects=True, vmem_limit_bytes=56 * 1024 * 1024
        ),
        name="gauss_newton",
    )(
        activations.T, act_tangent.T, kernel, kernel_tangent, slope, curvature,
        jnp.asarray(row_masks()), jnp.asarray(lane_masks()),
    )


def solution(mesh):
    return jax.shard_map(
        per_device,
        mesh=mesh,
        in_specs=(
            P(None, ("chan", "filt")),
            P(None, ("chan", "filt")),
            P(None, "chan", "filt"),
            P(None, "chan", "filt"),
            P("chan", "filt"),
            P("chan", "filt"),
        ),
        out_specs=(P("filt", "chan"), P(None, "chan", "filt")),
        check_vma=False,
    )
```

time: 274 us -> 75.7 us (0.28)
  waiting for transfers between devices: 91.7 us -> 0 us
  Pallas kernels: 0 us -> 71.5 us
  local copies, waits for them, and re-layouts: 74.6 us -> 3.32 us
  blocking collectives: 54.4 us -> 0 us
  matrix products: 25.3 us -> 0 us
  between operations: 14.6 us -> 0.64 us
  other arithmetic: 5.89 us -> 0 us
  starting transfers between devices: 4.57 us -> 0 us
    pallas_call x0 -> x1, Pallas kernels: none -> 71.5 us  [per_device(): pl.pallas_call(body, out_shape=(jax.ShapeDtypeStruct((SHARE, 128), BF), j...]
    all_gather x1 -> x0, waiting for transfers between devices: 65.7 us -> none  [gather_turned(): out = lax.all_gather(both, axis, axis=0, tiled=True)]
    all_to_all x2 -> x0, blocking collectives: 54.4 us -> none  [the longest x1 37.2 us: summed_on_arrival(): tiles = lax.all_to_all(split_up(x, dim, devices), axis, 0, 0, tiled=True)]
    reshape x29 -> x0, local copies, waits for them, and re-layouts: 45.9 us -> none  [the longest x25 40.7 us: windows(): result.append(padded[:, top:top + HH, left:left + WW, :].reshape(-1, width))]
    all_to_all x1 -> x0, waiting for transfers between devices: 26 us -> none  [summed_on_arrival(): tiles = lax.all_to_all(split_up(x, dim, devices), axis, 0, 0, tiled=True)]
    dot_general x36 -> x0, matrix products: 25.3 us -> none  [the longest x9 13.3 us: per_device(): lax.dot_general(backs[tap], kernel[tap], (((1,), (1,)), ((), ())), prefer...]
    slice x3 -> x0, local copies, waits for them, and re-layouts: 15.9 us -> none  [windows(): result.append(padded[:, top:top + HH, left:left + WW, :].reshape(-1, width))]
    unnamed x58 -> x2, local copies, waits for them, and re-layouts: 9.35 us -> 3.32 us
  transfers between devices with their start and end apart: 2 -> 0, of which waited for: 2 -> 0; matrix products, arithmetic and copies ran while one was open for 2% -> 0% of each run, Pallas kernels for 0% -> 0%
where the time goes in v1:
time: 75.7 us; the launch traced here: 75.5 us
  Pallas kernels  71.5 us (94%)
  local copies, waits for them, and re-layouts  3.32 us (4%)
    pallas_call x1, Pallas kernels, per_device(): pl.pallas_call(body, out_shape=(jax.ShapeDtypeStruct((SHARE, 128), BF), j...  71.5 us
    unnamed x2, local copies, waits for them, and re-layouts  3.32 us

profile of v1, /device:TPU:1, one launch (start us, length us, event | category | flops | bytes accessed | tf_op | source)
XLA Modules:
  0.0 75.5 jit_solution(11175887919905946470)
XLA Ops:
  0.6 71.5 %gauss_newton.1 = (bf16[162,128]{1,0:T(8,128)(2,1)}, f32[9,128,128]{2,1,0:T(8,128)}) custom-call(bf16[8,2592]{1,0:T(8,128)(2,1)} %bitcast.2, bf16[8,2592]{1,0:T(8,128)(2,1)} %bitcast.3, bf16[9,128,128]{2,1,0:T(8,128)(2,1)} %w_ref.1, bf16[9,128,128]{2,1,0:T(8,128)(2,1)} %v_ref.1, bf16[162,128]{1,0:T(8,128)(2,1)} %slope_ref.1, bf16[162,128]{1,0:T(8,128)(2,1)} %curv_ref.1, ...), custom_call_target="tpu_custom_call" | custom-call | tf_op jit(solution)/shard_map/gauss_newton/pallas_call | solution.py:393
  72.2 1.4 %copy.12 = bf16[162,128]{1,0:T(8,128)(2,1)} copy(bf16[162,128]{1,0:T(8,128)(2,1)} %get-tuple-element.4) | data formatting | bytes 82944
  73.6 1.9 %copy.13 = f32[9,128,128]{2,1,0:T(8,128)} copy(f32[9,128,128]{2,1,0:T(8,128)} %get-tuple-element.5) | data formatting | bytes 1179648

commit v2 on v1

--- a/solution.py
+++ b/solution.py
@@ -44,7 +44,7 @@
     cot_ref, kp_ref,
     gath, wcat, taps, xts, w32, w16, sib_out, sib_in, red_out, red_in, own,
     wgt, cx_out, cx_in, cz_out, cz_in,
-    a_ss, a_rs, p_rs, s_ss, s_rs, b_ss, b_rs, w_ss, w_rs, x_ss, x_rs, d_ss, d_rs,
+    a_ss, lo_rs, hi_rs, s_ss, s_rs, b_ss, b_rs, w_ss, w_rs, x_ss, x_rs, d_ss, d_rs,
 ):
     chan = lax.axis_index("chan")
     filt = lax.axis_index("filt")
@@ -62,11 +62,21 @@
     def z_dev(d):
         return {"chan": chan, "filt": half * 8 + at_z(d)}
 
-    def chip_at(d):
-        return lax.rem(chip + d + 8, 8)
-
-    def chip_dev(d):
-        return {"chan": 2 * chip_at(d) + core, "filt": filt}
+    def chip_at(j, sign=1):
+        row = lax.rem(lax.div(chip, 2) + sign * lax.div(j, 2) + 4, 4)
+        return 2 * row + lax.rem(chip + j, 2)
+
+    def chip_dev(j):
+        return {"chan": 2 * chip_at(j) + core, "filt": filt}
+
+    def turns(i, middle):
+        return middle + (1 - 2 * lax.rem(i, 2)) * lax.div(i + 1, 2)
+
+    def chip_turn(i):
+        return 2 * turns(lax.rem(i, 4), 2) + 1 - lax.div(i, 4)
+
+    def z_turn(i):
+        return turns(i, 4)
 
     def remote(src, dst, ss, rs, dev):
         return pltpu.make_async_remote_copy(
@@ -76,7 +86,7 @@
 
     barrier = pltpu.get_barrier_semaphore()
     peers = [sibling, across]
-    peers += [z_dev(d) for d in range(1, 8)] + [chip_dev(d) for d in range(1, 8)]
+    peers += [z_dev(d) for d in range(1, 8)] + [chip_dev(jnp.int32(d)) for d in range(1, 8)]
     for dev in peers:
         pl.semaphore_signal(barrier, inc=1, device_id=dev, device_id_type=pl.DeviceIdType.MESH)
 
@@ -87,45 +97,28 @@
 
     mine = half * 8
     theirs = (1 - half) * 8
+    right, left = z_dev(1), z_dev(-1)
     sent = []
-
-    def send_full(slot, dev):
-        n = len(sent)
-        c = remote(gath.at[slot], gath.at[slot], a_ss.at[n], a_rs.at[slot], dev)
-        c.start()
-        sent.append(c)
-
-    def low(slot):
-        return gath.at[slot, :, pl.ds(0, CUT)]
-
-    def high(slot):
-        return gath.at[slot, :, pl.ds(CUT, LANES - CUT)]
-
-    def send_low(slot, dev):
-        n = len(sent)
-        c = remote(low(slot), low(slot), a_ss.at[n], a_rs.at[slot], dev)
-        c.start()
-        sent.append(c)
-
-    def send_high(slot, dev):
-        n = len(sent)
-        c = remote(high(slot), high(slot), a_ss.at[n], p_rs.at[slot], dev)
-        c.start()
-        sent.append(c)
-
-    def got_full(slot):
-        remote(gath.at[slot], gath.at[slot], a_ss.at[0], a_rs.at[slot], across).wait_recv()
-
-    def got_low(slot):
-        remote(low(slot), low(slot), a_ss.at[0], a_rs.at[slot], across).wait_recv()
-
-    def got_high(slot):
-        remote(high(slot), high(slot), a_ss.at[0], p_rs.at[slot], across).wait_recv()
-
-    right, left = z_dev(1), z_dev(-1)
-    send_full(filt, right)
-    send_full(filt, left)
-    send_full(filt, across)
+    LOW, HIGH = pl.ds(0, CUT), pl.ds(CUT, LANES - CUT)
+
+    def piece(slot, lanes, n, dev):
+        ref = gath.at[slot, :, lanes]
+        sem = lo_rs if lanes is LOW else hi_rs
+        return remote(ref, ref, a_ss.at[n], sem.at[slot], dev)
+
+    def send(slot, lanes, *devs):
+        for dev in devs:
+            c = piece(slot, lanes, len(sent), dev)
+            c.start()
+            sent.append(c)
+
+    def got(slot, lanes):
+        piece(slot, lanes, 0, across).wait_recv()
+
+    send(filt, LOW, across)
+    send(filt, HIGH, right, left)
+    send(filt, LOW, right, left)
+    send(filt, HIGH, across)
 
     for k in range(TAPS):
         vk = v_ref[k].astype(F32).reshape(16, 1, 8, 128)
@@ -135,36 +128,29 @@
         )
         taps[k, 0:PAD, :] = jnp.zeros((PAD, 128), F32)
 
-    for h in range(1, 6):
-        if h <= 4:
-            slot = mine + at_z(-h)
-            got_full(slot)
+    got(theirs + z, LOW)
+    send(theirs + z, LOW, right, left)
+    for h in range(1, 5):
+        slot = mine + at_z(-h)
+        got(slot, HIGH)
+        if h < 4:
+            send(slot, HIGH, right)
+        send(slot, HIGH, across)
+        if h < 4:
+            slot = mine + at_z(h)
+            got(slot, HIGH)
+            if h < 3:
+                send(slot, HIGH, left)
+            send(slot, HIGH, across)
+        for group in (mine, theirs):
+            slot = group + at_z(h)
+            got(slot, LOW)
             if h < 4:
-                send_full(slot, right)
-            send_high(slot, across)
-        if h <= 3:
-            slot = mine + at_z(h)
-            got_full(slot)
-            if h < 3:
-                send_full(slot, left)
-            send_high(slot, across)
-        if h == 1:
-            slot = theirs + z
-            got_full(slot)
-            send_low(slot, right)
-            send_low(slot, left)
-        else:
-            slot = theirs + at_z(-(h - 1))
-            got_low(slot)
-            if h - 1 < 4:
-                send_low(slot, right)
-            if h - 1 <= 3:
-                slot = theirs + at_z(h - 1)
-                got_low(slot)
-                if h - 1 < 3:
-                    send_low(slot, left)
-    for d in range(1, 8):
-        got_high(theirs + at_z(d))
+                send(slot, LOW, left)
+                slot = group + at_z(-h)
+                got(slot, LOW)
+                if h < 3:
+                    send(slot, LOW, right)
 
     def forward(t, _):
         lanes = pl.ds(pl.multiple_of(t * BLOCK, 128), BLOCK)
@@ -177,7 +163,11 @@
                 taps[k + q, rows, :] = res[:, 128 * q:128 * q + 128]
         return 0
 
-    lax.fori_loop(0, LANES // BLOCK, forward, 0)
+    lax.fori_loop(0, CUT // BLOCK, forward, 0)
+    got(theirs + z, HIGH)
+    for h in range(1, 8):
+        got(theirs + at_z(h), HIGH)
+    lax.fori_loop(CUT // BLOCK, LANES // BLOCK, forward, 0)
 
     def combined(c, flip, put):
         start = c * SHARE
@@ -208,7 +198,7 @@
         return remote(sib_out.at[d], sib_in.at[d], s_ss.at[d], s_rs.at[d], sibling)
 
     def to_sibling(j, _):
-        d = chip_at(j + 1)
+        d = chip_at(chip_turn(j))
 
         def put(s, n, acc):
             sib_out[d, s:s + n, :] = acc
@@ -223,7 +213,8 @@
         d = chip_at(j)
         return remote(red_out.at[j], red_in.at[j], b_ss.at[j], b_rs.at[j], chip_dev(j))
 
-    def to_chip(j, _):
+    def to_chip(i, _):
+        j = chip_turn(i)
         d = chip_at(j)
         sib_copy(d).wait_recv()
 
@@ -234,7 +225,7 @@
         red_copy(j).start()
         return 0
 
-    lax.fori_loop(1, 8, to_chip, 0)
+    lax.fori_loop(0, 7, to_chip, 0)
     sib_copy(chip).wait_recv()
 
     def put_own(s, n, acc):
@@ -256,12 +247,13 @@
 
     lax.fori_loop(0, 8, shift, 0)
 
-    def add_in(j, _):
+    def add_in(i, _):
+        j = chip_turn(i)
         red_copy(j).wait_recv()
         own[...] += red_in[j].astype(F32)
         return 0
 
-    lax.fori_loop(1, 8, add_in, 0)
+    lax.fori_loop(0, 7, add_in, 0)
     slope = slope_ref[...].astype(F32)
     weighted = slope * slope * curv_ref[...].astype(F32) * own[0:SHARE, :]
     weighted = jnp.concatenate([weighted, jnp.zeros((ROWS - SHARE, 128), F32)], axis=0)
@@ -270,23 +262,25 @@
     def wgt_copy(slot, n, dev):
         return remote(wgt.at[slot], wgt.at[slot], w_ss.at[n], w_rs.at[slot], dev)
 
-    def spread(j, _):
+    def spread(i, _):
+        j = chip_turn(i)
         wgt_copy(chan, j, chip_dev(j)).start()
         return 0
 
-    lax.fori_loop(1, 8, spread, 0)
+    lax.fori_loop(0, 7, spread, 0)
     wgt_copy(chan, 0, sibling).start()
 
-    def pass_on(j, _):
-        slot = 2 * chip_at(-j) + core
+    def pass_on(i, _):
+        j = chip_turn(i)
+        slot = 2 * chip_at(j, -1) + core
         wgt_copy(slot, 0, sibling).wait_recv()
         wgt_copy(slot, 7 + j, sibling).start()
         return 0
 
-    lax.fori_loop(1, 8, pass_on, 0)
+    lax.fori_loop(0, 7, pass_on, 0)
 
     def from_sibling(j, _):
-        wgt_copy(2 * chip_at(-j) + other, 0, sibling).wait_recv()
+        wgt_copy(2 * chip_at(j) + other, 0, sibling).wait_recv()
         return 0
 
     lax.fori_loop(0, 8, from_sibling, 0)
@@ -319,8 +313,8 @@
     def cz_copy(j):
         return remote(cz_out.at[j], cz_in.at[j], d_ss.at[j], d_rs.at[j], z_dev(j))
 
-    def to_across(j, _):
-        j = lax.rem(j + 1, 8)
+    def to_across(i, _):
+        j = z_turn(i)
 
         def put(s, n, acc):
             cx_out[j, s:s + n, :] = acc.astype(BF)
@@ -331,7 +325,8 @@
 
     lax.fori_loop(0, 8, to_across, 0)
 
-    def to_z(j, _):
+    def to_z(i, _):
+        j = z_turn(i)
         cx_copy(j).wait_recv()
 
         def put(s, n, acc):
@@ -341,7 +336,7 @@
         cz_copy(j).start()
         return 0
 
-    lax.fori_loop(1, 8, to_z, 0)
+    lax.fori_loop(0, 7, to_z, 0)
     cx_copy(0).wait_recv()
 
     def put_last(s, n, acc):
@@ -358,12 +353,13 @@
 
     lax.fori_loop(0, TAPS, product, 0)
 
-    def add_z(j, _):
+    def add_z(i, _):
+        j = z_turn(i)
         cz_copy(j).wait_recv()
         own[...] += cz_in[j].astype(F32)
         return 0
 
-    lax.fori_loop(1, 8, add_z, 0)
+    lax.fori_loop(0, 7, add_z, 0)
     cot_ref[...] = own[0:SHARE, :].astype(BF)
 
     for c in sent:
@@ -415,7 +411,7 @@
             pltpu.VMEM(share, BF),
             pltpu.VMEM(share, BF),
             pltpu.VMEM(share, BF),
-            dma((24,)), dma((16,)), dma((16,)),
+            dma((32,)), dma((16,)), dma((16,)),
             dma((8,)), dma((8,)), dma((8,)), dma((8,)),
             dma((16,)), dma((16,)), dma((8,)), dma((8,)), dma((8,)), dma((8,)),
         ],

time: 75.7 us -> 70.8 us (0.935)
  Pallas kernels: 71.5 us -> 66.7 us
    pallas_call x1, Pallas kernels: 71.5 us -> 66.7 us  [per_device(): pl.pallas_call(body, out_shape=(jax.ShapeDtypeStruct((SHARE, 128), BF), j...]
where the time goes in v2:
time: 70.8 us; the launch traced here: 70.6 us
  Pallas kernels  66.7 us (94%)
  local copies, waits for them, and re-layouts  3.32 us (5%)
    pallas_call x1, Pallas kernels, per_device(): pl.pallas_call(body, out_shape=(jax.ShapeDtypeStruct((SHARE, 128), BF), j...  66.7 us
    unnamed x2, local copies, waits for them, and re-layouts  3.32 us

profile of v2, /device:TPU:1, one launch (start us, length us, event | category | flops | bytes accessed | tf_op | source)
XLA Modules:
  0.0 70.6 jit_solution(10791729996931031256)
XLA Ops:
  0.6 66.7 %gauss_newton.1 = (bf16[162,128]{1,0:T(8,128)(2,1)}, f32[9,128,128]{2,1,0:T(8,128)}) custom-call(bf16[8,2592]{1,0:T(8,128)(2,1)} %bitcast.2, bf16[8,2592]{1,0:T(8,128)(2,1)} %bitcast.3, bf16[9,128,128]{2,1,0:T(8,128)(2,1)} %w_ref.1, bf16[9,128,128]{2,1,0:T(8,128)(2,1)} %v_ref.1, bf16[162,128]{1,0:T(8,128)(2,1)} %slope_ref.1, bf16[162,128]{1,0:T(8,128)(2,1)} %curv_ref.1, ...), custom_call_target="tpu_custom_call" | custom-call | tf_op jit(solution)/shard_map/gauss_newton/pallas_call | solution.py:389
  67.3 1.4 %copy.12 = bf16[162,128]{1,0:T(8,128)(2,1)} copy(bf16[162,128]{1,0:T(8,128)(2,1)} %get-tuple-element.4) | data formatting | bytes 82944
  68.7 1.9 %copy.13 = f32[9,128,128]{2,1,0:T(8,128)} copy(f32[9,128,128]{2,1,0:T(8,128)} %get-tuple-element.5) | data formatting | bytes 1179648

commit v3 on v2

--- a/solution.py
+++ b/solution.py
@@ -40,10 +40,12 @@
 
 
 def body(
-    acts_ref, tans_ref, w_ref, v_ref, slope_ref, curv_ref, rmask, lmask,
-    cot_ref, kp_ref,
+    acts_ref, tans_ref, w_hbm, v_hbm, slope_hbm, curv_hbm, rmask_hbm, lmask_hbm,
+    cot_ref, kp_hbm,
+    w_ref, v_ref, slope_ref, curv_ref, rmask, lmask, kp_ref,
     gath, wcat, taps, xts, w32, w16, sib_out, sib_in, red_out, red_in, own,
     wgt, cx_out, cx_in, cz_out, cz_in,
+    l_s, k_s,
     a_ss, lo_rs, hi_rs, s_ss, s_rs, b_ss, b_rs, w_ss, w_rs, x_ss, x_rs, d_ss, d_rs,
 ):
     chan = lax.axis_index("chan")
@@ -62,6 +64,9 @@
     def z_dev(d):
         return {"chan": chan, "filt": half * 8 + at_z(d)}
 
+    def diag_dev(d):
+        return {"chan": chan, "filt": (1 - half) * 8 + at_z(d)}
+
     def chip_at(j, sign=1):
         row = lax.rem(lax.div(chip, 2) + sign * lax.div(j, 2) + 4, 4)
         return 2 * row + lax.rem(chip + j, 2)
@@ -85,10 +90,18 @@
         )
 
     barrier = pltpu.get_barrier_semaphore()
-    peers = [sibling, across]
+    peers = [sibling, across, diag_dev(1), diag_dev(-1)]
     peers += [z_dev(d) for d in range(1, 8)] + [chip_dev(jnp.int32(d)) for d in range(1, 8)]
     for dev in peers:
         pl.semaphore_signal(barrier, inc=1, device_id=dev, device_id_type=pl.DeviceIdType.MESH)
+
+    pairs = [
+        (v_hbm, v_ref), (w_hbm, w_ref), (rmask_hbm, rmask),
+        (slope_hbm, slope_ref), (curv_hbm, curv_ref), (lmask_hbm, lmask),
+    ]
+    loads = [pltpu.make_async_copy(src, dst, l_s.at[n]) for n, (src, dst) in enumerate(pairs)]
+    for c in loads:
+        c.start()
 
     both = jnp.concatenate([acts_ref[...].astype(F32), tans_ref[...].astype(F32)], axis=0)
     both = jnp.concatenate([both, jnp.zeros((16, LANES - PIXELS), F32)], axis=1)
@@ -115,11 +128,13 @@
     def got(slot, lanes):
         piece(slot, lanes, 0, across).wait_recv()
 
-    send(filt, LOW, across)
+    send(filt, LOW, diag_dev(1), diag_dev(-1))
     send(filt, HIGH, right, left)
-    send(filt, LOW, right, left)
+    send(filt, LOW, right, left, across)
     send(filt, HIGH, across)
 
+    for c in loads:
+        c.wait()
     for k in range(TAPS):
         vk = v_ref[k].astype(F32).reshape(16, 1, 8, 128)
         wk = w_ref[k].astype(F32).reshape(16, 1, 8, 128)
@@ -128,15 +143,14 @@
         )
         taps[k, 0:PAD, :] = jnp.zeros((PAD, 128), F32)
 
-    got(theirs + z, LOW)
-    send(theirs + z, LOW, right, left)
     for h in range(1, 5):
         slot = mine + at_z(-h)
         got(slot, HIGH)
         if h < 4:
             send(slot, HIGH, right)
-        send(slot, HIGH, across)
-        if h < 4:
+            if h == 3:
+                send(slot, HIGH, diag_dev(1))
+            send(slot, HIGH, across)
             slot = mine + at_z(h)
             got(slot, HIGH)
             if h < 3:
@@ -151,6 +165,8 @@
                 got(slot, LOW)
                 if h < 3:
                     send(slot, LOW, right)
+
+    got(theirs + z, LOW)
 
     def forward(t, _):
         lanes = pl.ds(pl.multiple_of(t * BLOCK, 128), BLOCK)
@@ -207,8 +223,6 @@
         sib_copy(d).start()
         return 0
 
-    lax.fori_loop(0, 8, to_sibling, 0)
-
     def red_copy(j):
         d = chip_at(j)
         return remote(red_out.at[j], red_in.at[j], b_ss.at[j], b_rs.at[j], chip_dev(j))
@@ -225,7 +239,13 @@
         red_copy(j).start()
         return 0
 
-    lax.fori_loop(0, 7, to_chip, 0)
+    def both_sends(i, _):
+        to_sibling(i + 1, 0)
+        to_chip(i, 0)
+        return 0
+
+    to_sibling(0, 0)
+    lax.fori_loop(0, 7, both_sends, 0)
     sib_copy(chip).wait_recv()
 
     def put_own(s, n, acc):
@@ -270,29 +290,34 @@
     lax.fori_loop(0, 7, spread, 0)
     wgt_copy(chan, 0, sibling).start()
 
+    def unpack(c):
+        start = c * SHARE
+        x = wgt[c].astype(F32)
+        w32[pl.ds(start, 160), :] = x[0:160]
+        w32[pl.ds(start + 160, 2), :] = x[160:162]
+
     def pass_on(i, _):
         j = chip_turn(i)
         slot = 2 * chip_at(j, -1) + core
         wgt_copy(slot, 0, sibling).wait_recv()
         wgt_copy(slot, 7 + j, sibling).start()
-        return 0
-
+        unpack(slot)
+        return 0
+
+    unpack(chan)
     lax.fori_loop(0, 7, pass_on, 0)
 
-    def from_sibling(j, _):
-        wgt_copy(2 * chip_at(j) + other, 0, sibling).wait_recv()
+    def from_sibling(i, _):
+        slot = 2 * chip_at(chip_turn(lax.rem(i + 7, 8)), -1) + other
+        wgt_copy(slot, 0, sibling).wait_recv()
+        unpack(slot)
         return 0
 
     lax.fori_loop(0, 8, from_sibling, 0)
-
-    def compact(c, _):
-        w32[pl.ds(c * SHARE, 168), :] = wgt[c, 0:168, :].astype(F32)
-        return 0
-
-    lax.fori_loop(0, 16, compact, 0)
     w32[PIXELS:LANES, :] = jnp.zeros((LANES - PIXELS, 128), F32)
 
-    def backward(t, _):
+    def backward(i, _):
+        t = lax.rem(i + 3 * (1 - half), LANES // BLOCK)
         rows = pl.ds(pl.multiple_of(t * BLOCK, 16), BLOCK)
         spot = pl.ds(pl.multiple_of(PAD + t * BLOCK, 16), BLOCK)
         w = w32[rows, :].astype(BF)
@@ -305,7 +330,16 @@
                 taps[k + q, spot, :] = res[:, 128 * q:128 * q + 128]
         return 0
 
-    lax.fori_loop(0, LANES // BLOCK, backward, 0)
+    lax.fori_loop(0, 4, backward, 0)
+
+    scale = F32(1.0) / jnp.sqrt(F32(PIXELS))
+
+    def kp_copy(k):
+        return pltpu.make_async_copy(kp_ref.at[k], kp_hbm.at[k], k_s.at[k])
+
+    def product(k):
+        kp_ref[k] = jnp.dot(xts[k], w16[...], preferred_element_type=F32) * scale
+        kp_copy(k).start()
 
     def cx_copy(j):
         return remote(cx_out.at[j], cx_in.at[j], x_ss.at[j], x_rs.at[j], across)
@@ -324,6 +358,8 @@
         return 0
 
     lax.fori_loop(0, 8, to_across, 0)
+
+    lax.fori_loop(4, LANES // BLOCK, backward, 0)
 
     def to_z(i, _):
         j = z_turn(i)
@@ -334,6 +370,7 @@
 
         combined(mine + at_z(j), True, put)
         cz_copy(j).start()
+        product(i)
         return 0
 
     lax.fori_loop(0, 7, to_z, 0)
@@ -344,14 +381,8 @@
 
     combined(mine + z, True, put_last)
 
-    scale = F32(1.0) / jnp.sqrt(F32(PIXELS))
-
-    def product(k, _):
-        res = jnp.dot(xts[k], w16[...], preferred_element_type=F32)
-        kp_ref[k] = res * scale
-        return 0
-
-    lax.fori_loop(0, TAPS, product, 0)
+    product(7)
+    product(8)
 
     def add_z(i, _):
         j = z_turn(i)
@@ -364,6 +395,8 @@
 
     for c in sent:
         c.wait_send()
+    for k in range(TAPS):
+        kp_copy(k).wait()
 
     def drain(j, _):
         sib_copy(j).wait_send()
@@ -382,19 +415,42 @@
     lax.fori_loop(1, 8, drain_far, 0)
 
 
+def settle(cot_in, kp_in, cot_ref, kp_ref, cot_v, kp_v, in_s, out_s):
+    legs = [(cot_in, cot_v, cot_ref)]
+    for n in range(3):
+        part = pl.ds(3 * n, 3)
+        legs.append((kp_in.at[part], kp_v.at[part], kp_ref.at[part]))
+    for n, (src, via, _) in enumerate(legs):
+        pltpu.make_async_copy(src, via, in_s.at[n]).start()
+    for n, (src, via, dst) in enumerate(legs):
+        pltpu.make_async_copy(src, via, in_s.at[n]).wait()
+        pltpu.make_async_copy(via, dst, out_s.at[n]).start()
+    for n, (_, via, dst) in enumerate(legs):
+        pltpu.make_async_copy(via, dst, out_s.at[n]).wait()
+
+
 def per_device(activations, act_tangent, kernel, kernel_tangent, slope, curvature):
     vm = pl.BlockSpec(memory_space=pltpu.VMEM)
+    hbm = pl.BlockSpec(memory_space=pl.ANY)
     dma = pltpu.SemaphoreType.DMA
     share = (8, ROWS, 128)
-    return pl.pallas_call(
+    shapes = (
+        jax.ShapeDtypeStruct((SHARE, 128), BF),
+        jax.ShapeDtypeStruct((TAPS, 128, 128), F32),
+    )
+    results = pl.pallas_call(
         body,
-        out_shape=(
-            jax.ShapeDtypeStruct((SHARE, 128), BF),
-            jax.ShapeDtypeStruct((TAPS, 128, 128), F32),
-        ),
-        in_specs=[vm] * 8,
-        out_specs=(vm, vm),
+        out_shape=shapes,
+        in_specs=[vm] * 2 + [hbm] * 6,
+        out_specs=(vm, hbm),
         scratch_shapes=[
+            pltpu.VMEM((TAPS, 128, 128), BF),
+            pltpu.VMEM((TAPS, 128, 128), BF),
+            pltpu.VMEM((SHARE, 128), BF),
+            pltpu.VMEM((SHARE, 128), BF),
+            pltpu.VMEM((4, IMAGE + ROWS, 128), F32),
+            pltpu.VMEM((16, LANES), F32),
+            pltpu.VMEM((TAPS, 128, 128), F32),
             pltpu.VMEM((16, 16, LANES), BF),
             pltpu.VMEM((256, TAPS * 128), BF),
             pltpu.VMEM((TAPS, PAD + LANES, 128), F32),
@@ -411,7 +467,8 @@
             pltpu.VMEM(share, BF),
             pltpu.VMEM(share, BF),
             pltpu.VMEM(share, BF),
-            dma((32,)), dma((16,)), dma((16,)),
+            dma((6,)), dma((TAPS,)),
+            dma((34,)), dma((16,)), dma((16,)),
             dma((8,)), dma((8,)), dma((8,)), dma((8,)),
             dma((16,)), dma((16,)), dma((8,)), dma((8,)), dma((8,)), dma((8,)),
         ],
@@ -423,6 +480,16 @@
         activations.T, act_tangent.T, kernel, kernel_tangent, slope, curvature,
         jnp.asarray(row_masks()), jnp.asarray(lane_masks()),
     )
+    return pl.pallas_call(
+        settle,
+        out_shape=shapes,
+        in_specs=[hbm, hbm],
+        out_specs=(hbm, hbm),
+        scratch_shapes=[
+            pltpu.VMEM((SHARE, 128), BF), pltpu.VMEM((TAPS, 128, 128), F32), dma((4,)), dma((4,))
+        ],
+        name="settle",
+    )(*results)
 
 
 def solution(mesh):

time: 70.8 us -> 67.5 us (0.953)
  local copies, waits for them, and re-layouts: 3.32 us -> 0 us
    unnamed x2 -> x0, local copies, waits for them, and re-layouts: 3.32 us -> none
    pallas_call x1 -> x2, Pallas kernels: 66.7 us -> 66.7 us  [the longest x1 64.8 us: per_device(): pl.pallas_call(body, out_shape=shapes, in_specs=[vm] * 2 + [hbm] * 6, out...]
where the time goes in v3:
time: 67.5 us; the launch traced here: 67.4 us
  Pallas kernels  66.7 us (99%)
    pallas_call x1, Pallas kernels, per_device(): pl.pallas_call(body, out_shape=shapes, in_specs=[vm] * 2 + [hbm] * 6, out...  64.8 us
    pallas_call x1, Pallas kernels, per_device(): pl.pallas_call(settle, out_shape=shapes, in_specs=[hbm, hbm], out_specs=(...  1.89 us

profile of v3, /device:TPU:1, one launch (start us, length us, event | category | flops | bytes accessed | tf_op | source)
XLA Modules:
  0.0 67.4 jit_solution(4217347598973864347)
XLA Ops:
  0.6 64.8 %gauss_newton.1 = (bf16[162,128]{1,0:T(8,128)(2,1)}, f32[9,128,128]{2,1,0:T(8,128)}) custom-call(bf16[8,2592]{1,0:T(8,128)(2,1)} %bitcast.2, bf16[8,2592]{1,0:T(8,128)(2,1)} %bitcast.3, bf16[9,128,128]{2,1,0:T(8,128)(2,1)} %w_hbm.1, bf16[9,128,128]{2,1,0:T(8,128)(2,1)} %v_hbm.1, bf16[162,128]{1,0:T(8,128)(2,1)} %slope_hbm.1, bf16[162,128]{1,0:T(8,128)(2,1)} %curv_hbm.1, ...), custom_call_target="tpu_custom_call" | custom-call | tf_op jit(solution)/shard_map/gauss_newton/pallas_call | solution.py:441
  65.5 1.9 %settle.1 = (bf16[162,128]{1,0:T(8,128)(2,1)}, f32[9,128,128]{2,1,0:T(8,128)}) custom-call(bf16[162,128]{1,0:T(8,128)(2,1)} %get-tuple-element.4.cot_in, f32[9,128,128]{2,1,0:T(8,128)} %get-tuple-element.5.kp_in), custom_call_target="tpu_custom_call" | custom-call | tf_op jit(solution)/shard_map/settle/pallas_call | solution.py:483

commit v4 on v3

--- a/solution.py
+++ b/solution.py
@@ -14,6 +14,7 @@
 CUT = 1152
 SHARE = 162
 ROWS = 176
+PARTS = ((0, 96), (96, 80))
 PAD = 16
 BLOCK = 384
 TAPS = 9
@@ -179,21 +180,22 @@
                 taps[k + q, rows, :] = res[:, 128 * q:128 * q + 128]
         return 0
 
-    lax.fori_loop(0, CUT // BLOCK, forward, 0)
+    lax.fori_loop(0, CUT // BLOCK, forward, 0, unroll=True)
     got(theirs + z, HIGH)
     for h in range(1, 8):
         got(theirs + at_z(h), HIGH)
-    lax.fori_loop(CUT // BLOCK, LANES // BLOCK, forward, 0)
-
-    def combined(c, flip, put):
+    lax.fori_loop(CUT // BLOCK, LANES // BLOCK, forward, 0, unroll=True)
+
+    def combined(c, flip, part, put):
         start = c * SHARE
         within = lax.rem(start, IMAGE)
-        step = ROWS // 2
-        for s in range(0, ROWS, step):
+        first, count = PARTS[part]
+        step = count // 2
+        for s in range(first, first + count, step):
             m = [rmask[n, pl.ds(within + s, step), :] for n in range(4)]
             acc = None
             for a in range(3):
-                part = None
+                row = None
                 for e in range(3):
                     k = 3 * a + e
                     off = WW * (a - 1) + e - 1
@@ -202,56 +204,65 @@
                         val = val * m[2]
                     if e == 2:
                         val = val * m[3]
-                    part = val if part is None else part + val
+                    row = val if row is None else row + val
                 if a == 0:
-                    part = part * m[0]
+                    row = row * m[0]
                 if a == 2:
-                    part = part * m[1]
-                acc = part if acc is None else acc + part
+                    row = row * m[1]
+                acc = row if acc is None else acc + row
             put(s, step, acc)
 
-    def sib_copy(d):
-        return remote(sib_out.at[d], sib_in.at[d], s_ss.at[d], s_rs.at[d], sibling)
-
-    def to_sibling(j, _):
-        d = chip_at(chip_turn(j))
+    def rows_of(part):
+        return pl.ds(*PARTS[part])
+
+    def sib_copy(d, part):
+        return remote(
+            sib_out.at[d, rows_of(part)], sib_in.at[d, rows_of(part)],
+            s_ss.at[2 * d + part], s_rs.at[2 * d + part], sibling,
+        )
+
+    def to_sibling(i, part):
+        d = chip_at(chip_turn(i))
 
         def put(s, n, acc):
             sib_out[d, s:s + n, :] = acc
 
-        combined(2 * d + other, False, put)
-        sib_copy(d).start()
-        return 0
-
-    def red_copy(j):
-        d = chip_at(j)
-        return remote(red_out.at[j], red_in.at[j], b_ss.at[j], b_rs.at[j], chip_dev(j))
-
-    def to_chip(i, _):
+        combined(2 * d + other, False, part, put)
+        sib_copy(d, part).start()
+
+    def red_copy(j, part):
+        return remote(
+            red_out.at[j, rows_of(part)], red_in.at[j, rows_of(part)],
+            b_ss.at[2 * j + part], b_rs.at[2 * j + part], chip_dev(j),
+        )
+
+    def to_chip(i, part):
         j = chip_turn(i)
         d = chip_at(j)
-        sib_copy(d).wait_recv()
+        sib_copy(d, part).wait_recv()
 
         def put(s, n, acc):
             red_out[j, s:s + n, :] = (acc + sib_in[d, s:s + n, :]).astype(BF)
 
-        combined(2 * d + core, False, put)
-        red_copy(j).start()
-        return 0
-
-    def both_sends(i, _):
-        to_sibling(i + 1, 0)
-        to_chip(i, 0)
-        return 0
-
-    to_sibling(0, 0)
-    lax.fori_loop(0, 7, both_sends, 0)
-    sib_copy(chip).wait_recv()
+        combined(2 * d + core, False, part, put)
+        red_copy(j, part).start()
+
+    for part in range(2):
+
+        def both_sends(i, _, part=part):
+            to_sibling(i + 1, part)
+            to_chip(i, part)
+            return 0
+
+        to_sibling(0, part)
+        lax.fori_loop(0, 7, both_sends, 0)
 
     def put_own(s, n, acc):
         own[s:s + n, :] = acc + sib_in[chip, s:s + n, :]
 
-    combined(2 * chip + core, False, put_own)
+    for part in range(2):
+        sib_copy(chip, part).wait_recv()
+        combined(2 * chip + core, False, part, put_own)
 
     def shift(t, _):
         g = gath[pl.ds(2 * t, 2)].astype(F32)
@@ -265,55 +276,72 @@
                 xts[k, rows, :] = (xk * lmask[k:k + 1, :]).astype(BF)
         return 0
 
-    lax.fori_loop(0, 8, shift, 0)
-
-    def add_in(i, _):
-        j = chip_turn(i)
-        red_copy(j).wait_recv()
-        own[...] += red_in[j].astype(F32)
-        return 0
-
-    lax.fori_loop(0, 7, add_in, 0)
-    slope = slope_ref[...].astype(F32)
-    weighted = slope * slope * curv_ref[...].astype(F32) * own[0:SHARE, :]
-    weighted = jnp.concatenate([weighted, jnp.zeros((ROWS - SHARE, 128), F32)], axis=0)
-    wgt[chan] = weighted.astype(BF)
-
-    def wgt_copy(slot, n, dev):
-        return remote(wgt.at[slot], wgt.at[slot], w_ss.at[n], w_rs.at[slot], dev)
-
-    def spread(i, _):
-        j = chip_turn(i)
-        wgt_copy(chan, j, chip_dev(j)).start()
-        return 0
-
-    lax.fori_loop(0, 7, spread, 0)
-    wgt_copy(chan, 0, sibling).start()
-
-    def unpack(c):
+    lax.fori_loop(0, 4, shift, 0)
+
+    def wgt_copy(slot, n, part, dev):
+        ref = wgt.at[slot, rows_of(part)]
+        return remote(ref, ref, w_ss.at[2 * n + part], w_rs.at[2 * slot + part], dev)
+
+    for part, (first, count) in enumerate(PARTS):
+        rows = slice(first, first + count)
+
+        def add_in(i, _, part=part, rows=rows):
+            j = chip_turn(i)
+            red_copy(j, part).wait_recv()
+            own[rows, :] += red_in[j, rows, :].astype(F32)
+            return 0
+
+        lax.fori_loop(0, 7, add_in, 0)
+        valid = min(first + count, SHARE) - first
+        slope = slope_ref[first:first + valid, :].astype(F32)
+        curv = curv_ref[first:first + valid, :].astype(F32)
+        weighted = slope * slope * curv * own[first:first + valid, :]
+        if valid < count:
+            weighted = jnp.concatenate([weighted, jnp.zeros((count - valid, 128), F32)], axis=0)
+        wgt[chan, rows, :] = weighted.astype(BF)
+
+        def spread(i, _, part=part):
+            j = chip_turn(i)
+            wgt_copy(chan, j, part, chip_dev(j)).start()
+            return 0
+
+        lax.fori_loop(0, 7, spread, 0)
+        wgt_copy(chan, 0, part, sibling).start()
+
+    lax.fori_loop(4, 8, shift, 0)
+
+    def unpack(c, part):
         start = c * SHARE
-        x = wgt[c].astype(F32)
-        w32[pl.ds(start, 160), :] = x[0:160]
-        w32[pl.ds(start + 160, 2), :] = x[160:162]
-
-    def pass_on(i, _):
-        j = chip_turn(i)
-        slot = 2 * chip_at(j, -1) + core
-        wgt_copy(slot, 0, sibling).wait_recv()
-        wgt_copy(slot, 7 + j, sibling).start()
-        unpack(slot)
-        return 0
-
-    unpack(chan)
-    lax.fori_loop(0, 7, pass_on, 0)
-
-    def from_sibling(i, _):
-        slot = 2 * chip_at(chip_turn(lax.rem(i + 7, 8)), -1) + other
-        wgt_copy(slot, 0, sibling).wait_recv()
-        unpack(slot)
-        return 0
-
-    lax.fori_loop(0, 8, from_sibling, 0)
+        first, count = PARTS[part]
+        x = wgt[c, rows_of(part), :].astype(F32)
+        if part == 0:
+            w32[pl.ds(start, 96), :] = x
+        else:
+            w32[pl.ds(start + 96, 64), :] = x[0:64]
+            w32[pl.ds(start + 160, 2), :] = x[64:66]
+
+    for part in range(2):
+
+        def pass_on(i, _, part=part):
+            j = chip_turn(i)
+            slot = 2 * chip_at(j, -1) + core
+            wgt_copy(slot, 0, part, sibling).wait_recv()
+            wgt_copy(slot, 7 + j, part, sibling).start()
+            unpack(slot, part)
+            return 0
+
+        unpack(chan, part)
+        lax.fori_loop(0, 7, pass_on, 0)
+
+    for part in range(2):
+
+        def from_sibling(i, _, part=part):
+            slot = 2 * chip_at(chip_turn(lax.rem(i + 7, 8)), -1) + other
+            wgt_copy(slot, 0, part, sibling).wait_recv()
+            unpack(slot, part)
+            return 0
+
+        lax.fori_loop(0, 8, from_sibling, 0)
     w32[PIXELS:LANES, :] = jnp.zeros((LANES - PIXELS, 128), F32)
 
     def backward(i, _):
@@ -330,7 +358,7 @@
                 taps[k + q, spot, :] = res[:, 128 * q:128 * q + 128]
         return 0
 
-    lax.fori_loop(0, 4, backward, 0)
+    lax.fori_loop(0, 4, backward, 0, unroll=True)
 
     scale = F32(1.0) / jnp.sqrt(F32(PIXELS))
 
@@ -341,11 +369,17 @@
         kp_ref[k] = jnp.dot(xts[k], w16[...], preferred_element_type=F32) * scale
         kp_copy(k).start()
 
-    def cx_copy(j):
-        return remote(cx_out.at[j], cx_in.at[j], x_ss.at[j], x_rs.at[j], across)
-
-    def cz_copy(j):
-        return remote(cz_out.at[j], cz_in.at[j], d_ss.at[j], d_rs.at[j], z_dev(j))
+    def cx_copy(j, part):
+        return remote(
+            cx_out.at[j, rows_of(part)], cx_in.at[j, rows_of(part)],
+            x_ss.at[2 * j + part], x_rs.at[2 * j + part], across,
+        )
+
+    def cz_copy(j, part):
+        return remote(
+            cz_out.at[j, rows_of(part)], cz_in.at[j, rows_of(part)],
+            d_ss.at[2 * j + part], d_rs.at[2 * j + part], z_dev(j),
+        )
 
     def to_across(i, _):
         j = z_turn(i)
@@ -353,40 +387,42 @@
         def put(s, n, acc):
             cx_out[j, s:s + n, :] = acc.astype(BF)
 
-        combined(theirs + at_z(j), True, put)
-        cx_copy(j).start()
+        for part in range(2):
+            combined(theirs + at_z(j), True, part, put)
+            cx_copy(j, part).start()
         return 0
 
     lax.fori_loop(0, 8, to_across, 0)
-
-    lax.fori_loop(4, LANES // BLOCK, backward, 0)
+    lax.fori_loop(4, LANES // BLOCK, backward, 0, unroll=True)
 
     def to_z(i, _):
         j = z_turn(i)
-        cx_copy(j).wait_recv()
 
         def put(s, n, acc):
             cz_out[j, s:s + n, :] = (acc + cx_in[j, s:s + n, :].astype(F32)).astype(BF)
 
-        combined(mine + at_z(j), True, put)
-        cz_copy(j).start()
+        for part in range(2):
+            cx_copy(j, part).wait_recv()
+            combined(mine + at_z(j), True, part, put)
+            cz_copy(j, part).start()
         product(i)
         return 0
 
     lax.fori_loop(0, 7, to_z, 0)
-    cx_copy(0).wait_recv()
 
     def put_last(s, n, acc):
         own[s:s + n, :] = acc + cx_in[0, s:s + n, :].astype(F32)
 
-    combined(mine + z, True, put_last)
-
+    for part in range(2):
+        cx_copy(0, part).wait_recv()
+        combined(mine + z, True, part, put_last)
     product(7)
     product(8)
 
     def add_z(i, _):
         j = z_turn(i)
-        cz_copy(j).wait_recv()
+        cz_copy(j, 0).wait_recv()
+        cz_copy(j, 1).wait_recv()
         own[...] += cz_in[j].astype(F32)
         return 0
 
@@ -399,17 +435,19 @@
         kp_copy(k).wait()
 
     def drain(j, _):
-        sib_copy(j).wait_send()
-        cx_copy(j).wait_send()
-        wgt_copy(chan, j, sibling).wait_send()
+        for part in range(2):
+            sib_copy(j, part).wait_send()
+            cx_copy(j, part).wait_send()
+            wgt_copy(chan, j, part, sibling).wait_send()
         return 0
 
     lax.fori_loop(0, 8, drain, 0)
 
     def drain_far(j, _):
-        red_copy(j).wait_send()
-        cz_copy(j).wait_send()
-        wgt_copy(chan, 7 + j, sibling).wait_send()
+        for part in range(2):
+            red_copy(j, part).wait_send()
+            cz_copy(j, part).wait_send()
+            wgt_copy(chan, 7 + j, part, sibling).wait_send()
         return 0
 
     lax.fori_loop(1, 8, drain_far, 0)
@@ -469,8 +507,8 @@
             pltpu.VMEM(share, BF),
             dma((6,)), dma((TAPS,)),
             dma((34,)), dma((16,)), dma((16,)),
-            dma((8,)), dma((8,)), dma((8,)), dma((8,)),
-            dma((16,)), dma((16,)), dma((8,)), dma((8,)), dma((8,)), dma((8,)),
+            dma((16,)), dma((16,)), dma((16,)), dma((16,)),
+            dma((32,)), dma((32,)), dma((16,)), dma((16,)), dma((16,)), dma((16,)),
         ],
         compiler_params=pltpu.CompilerParams(
             collective_id=0, has_side_effects=True, vmem_limit_bytes=56 * 1024 * 1024

time: 67.5 us -> 68.1 us (level)
  no operation moved by 1% of the time
where the time goes in v4:
time: 68.1 us; the launch traced here: 67.9 us
  Pallas kernels  67.3 us (99%)
    pallas_call x1, Pallas kernels, per_device(): pl.pallas_call(body, out_shape=shapes, in_specs=[vm] * 2 + [hbm] * 6, out...  65.4 us
    pallas_call x1, Pallas kernels, per_device(): pl.pallas_call(settle, out_shape=shapes, in_specs=[hbm, hbm], out_specs=(...  1.89 us

profile of v4, /device:TPU:1, one launch (start us, length us, event | category | flops | bytes accessed | tf_op | source)
XLA Modules:
  0.0 67.9 jit_solution(2116565209415520278)
XLA Ops:
  0.6 65.4 %gauss_newton.1 = (bf16[162,128]{1,0:T(8,128)(2,1)}, f32[9,128,128]{2,1,0:T(8,128)}) custom-call(bf16[8,2592]{1,0:T(8,128)(2,1)} %bitcast.2, bf16[8,2592]{1,0:T(8,128)(2,1)} %bitcast.3, bf16[9,128,128]{2,1,0:T(8,128)(2,1)} %w_hbm.1, bf16[9,128,128]{2,1,0:T(8,128)(2,1)} %v_hbm.1, bf16[162,128]{1,0:T(8,128)(2,1)} %slope_hbm.1, bf16[162,128]{1,0:T(8,128)(2,1)} %curv_hbm.1, ...), custom_call_target="tpu_custom_call" | custom-call | tf_op jit(solution)/shard_map/gauss_newton/pallas_call | solution.py:479
  66.1 1.9 %settle.1 = (bf16[162,128]{1,0:T(8,128)(2,1)}, f32[9,128,128]{2,1,0:T(8,128)}) custom-call(bf16[162,128]{1,0:T(8,128)(2,1)} %get-tuple-element.4.cot_in, f32[9,128,128]{2,1,0:T(8,128)} %get-tuple-element.5.kp_in), custom_call_target="tpu_custom_call" | custom-call | tf_op jit(solution)/shard_map/settle/pallas_call | solution.py:521

commit v5 on v4

--- a/solution.py
+++ b/solution.py
@@ -247,15 +247,25 @@
         combined(2 * d + core, False, part, put)
         red_copy(j, part).start()
 
-    for part in range(2):
-
-        def both_sends(i, _, part=part):
-            to_sibling(i + 1, part)
-            to_chip(i, part)
+    def ahead(first, last, part, step=None, chip_part=None):
+        def go(i, _):
+            to_sibling(i, part)
+            if step is not None:
+                to_chip(i + step, chip_part)
             return 0
 
-        to_sibling(0, part)
-        lax.fori_loop(0, 7, both_sends, 0)
+        lax.fori_loop(first, last, go, 0)
+
+    def behind(i, _):
+        to_chip(i, 1)
+        return 0
+
+    ahead(0, 4, 0)
+    ahead(4, 8, 0, -4, 0)
+    ahead(0, 3, 1, 4, 0)
+    ahead(3, 4, 1)
+    ahead(4, 8, 1, -4, 1)
+    lax.fori_loop(4, 7, behind, 0)
 
     def put_own(s, n, acc):
         own[s:s + n, :] = acc + sib_in[chip, s:s + n, :]

time: 68.1 us -> 64.9 us (0.953)
  Pallas kernels: 67.3 us -> 64.1 us
    pallas_call x1, Pallas kernels: 65.4 us -> 62.2 us  [per_device(): pl.pallas_call(body, out_shape=shapes, in_specs=[vm] * 2 + [hbm] * 6, out...]
where the time goes in v5:
time: 64.9 us; the launch traced here: 64.7 us
  Pallas kernels  64.1 us (99%)
    pallas_call x1, Pallas kernels, per_device(): pl.pallas_call(body, out_shape=shapes, in_specs=[vm] * 2 + [hbm] * 6, out...  62.2 us
    pallas_call x1, Pallas kernels, per_device(): pl.pallas_call(settle, out_shape=shapes, in_specs=[hbm, hbm], out_specs=(...  1.89 us

profile of v5, /device:TPU:1, one launch (start us, length us, event | category | flops | bytes accessed | tf_op | source)
XLA Modules:
  0.0 64.7 jit_solution(16959390490675618777)
XLA Ops:
  0.6 62.2 %gauss_newton.1 = (bf16[162,128]{1,0:T(8,128)(2,1)}, f32[9,128,128]{2,1,0:T(8,128)}) custom-call(bf16[8,2592]{1,0:T(8,128)(2,1)} %bitcast.2, bf16[8,2592]{1,0:T(8,128)(2,1)} %bitcast.3, bf16[9,128,128]{2,1,0:T(8,128)(2,1)} %w_hbm.1, bf16[9,128,128]{2,1,0:T(8,128)(2,1)} %v_hbm.1, bf16[162,128]{1,0:T(8,128)(2,1)} %slope_hbm.1, bf16[162,128]{1,0:T(8,128)(2,1)} %curv_hbm.1, ...), custom_call_target="tpu_custom_call" | custom-call | tf_op jit(solution)/shard_map/gauss_newton/pallas_call | solution.py:489
  62.8 1.9 %settle.1 = (bf16[162,128]{1,0:T(8,128)(2,1)}, f32[9,128,128]{2,1,0:T(8,128)}) custom-call(bf16[162,128]{1,0:T(8,128)(2,1)} %get-tuple-element.4.cot_in, f32[9,128,128]{2,1,0:T(8,128)} %get-tuple-element.5.kp_in), custom_call_target="tpu_custom_call" | custom-call | tf_op jit(solution)/shard_map/settle/pallas_call | solution.py:531

commit v6 on v5

--- a/solution.py
+++ b/solution.py
@@ -47,7 +47,7 @@
     gath, wcat, taps, xts, w32, w16, sib_out, sib_in, red_out, red_in, own,
     wgt, cx_out, cx_in, cz_out, cz_in,
     l_s, k_s,
-    a_ss, lo_rs, hi_rs, s_ss, s_rs, b_ss, b_rs, w_ss, w_rs, x_ss, x_rs, d_ss, d_rs,
+    send_s, lo_rs, hi_rs, far_rs, s_rs, b_rs, w_rs, p_rs, x_rs, d_rs,
 ):
     chan = lax.axis_index("chan")
     filt = lax.axis_index("filt")
@@ -112,27 +112,28 @@
     mine = half * 8
     theirs = (1 - half) * 8
     right, left = z_dev(1), z_dev(-1)
-    sent = []
     LOW, HIGH = pl.ds(0, CUT), pl.ds(CUT, LANES - CUT)
 
-    def piece(slot, lanes, n, dev):
+    def piece(slot, lanes, sem, dev):
         ref = gath.at[slot, :, lanes]
-        sem = lo_rs if lanes is LOW else hi_rs
-        return remote(ref, ref, a_ss.at[n], sem.at[slot], dev)
-
-    def send(slot, lanes, *devs):
+        return remote(ref, ref, send_s.at[0], sem, dev)
+
+    def send(slot, lanes, *devs, cross=False):
         for dev in devs:
-            c = piece(slot, lanes, len(sent), dev)
-            c.start()
-            sent.append(c)
+            if cross:
+                sem = far_rs.at[0]
+            else:
+                sem = lo_rs.at[slot] if lanes is LOW else hi_rs.at[lax.rem(slot, 8)]
+            piece(slot, lanes, sem, dev).start()
 
     def got(slot, lanes):
-        piece(slot, lanes, 0, across).wait_recv()
+        sem = lo_rs.at[slot] if lanes is LOW else hi_rs.at[lax.rem(slot, 8)]
+        piece(slot, lanes, sem, across).wait_recv()
 
     send(filt, LOW, diag_dev(1), diag_dev(-1))
     send(filt, HIGH, right, left)
     send(filt, LOW, right, left, across)
-    send(filt, HIGH, across)
+    send(filt, HIGH, across, cross=True)
 
     for c in loads:
         c.wait()
@@ -150,13 +151,13 @@
         if h < 4:
             send(slot, HIGH, right)
             if h == 3:
-                send(slot, HIGH, diag_dev(1))
-            send(slot, HIGH, across)
+                send(slot, HIGH, diag_dev(1), cross=True)
+            send(slot, HIGH, across, cross=True)
             slot = mine + at_z(h)
             got(slot, HIGH)
             if h < 3:
                 send(slot, HIGH, left)
-            send(slot, HIGH, across)
+            send(slot, HIGH, across, cross=True)
         for group in (mine, theirs):
             slot = group + at_z(h)
             got(slot, LOW)
@@ -181,9 +182,8 @@
         return 0
 
     lax.fori_loop(0, CUT // BLOCK, forward, 0, unroll=True)
-    got(theirs + z, HIGH)
-    for h in range(1, 8):
-        got(theirs + at_z(h), HIGH)
+    cross = gath.at[pl.ds(theirs, 8), :, HIGH]
+    remote(cross, cross, send_s.at[0], far_rs.at[0], across).wait_recv()
     lax.fori_loop(CUT // BLOCK, LANES // BLOCK, forward, 0, unroll=True)
 
     def combined(c, flip, part, put):
@@ -218,7 +218,7 @@
     def sib_copy(d, part):
         return remote(
             sib_out.at[d, rows_of(part)], sib_in.at[d, rows_of(part)],
-            s_ss.at[2 * d + part], s_rs.at[2 * d + part], sibling,
+            send_s.at[1], s_rs.at[2 * d + part], sibling,
         )
 
     def to_sibling(i, part):
@@ -233,7 +233,7 @@
     def red_copy(j, part):
         return remote(
             red_out.at[j, rows_of(part)], red_in.at[j, rows_of(part)],
-            b_ss.at[2 * j + part], b_rs.at[2 * j + part], chip_dev(j),
+            send_s.at[2], b_rs.at[part], chip_dev(j),
         )
 
     def to_chip(i, part):
@@ -288,35 +288,37 @@
 
     lax.fori_loop(0, 4, shift, 0)
 
-    def wgt_copy(slot, n, part, dev):
+    def wgt_copy(slot, part, dev):
         ref = wgt.at[slot, rows_of(part)]
-        return remote(ref, ref, w_ss.at[2 * n + part], w_rs.at[2 * slot + part], dev)
+        return remote(ref, ref, send_s.at[3], w_rs.at[2 * lax.div(slot, 2) + part], dev)
+
+    def sib_wgt_copy(slot, part):
+        ref = wgt.at[slot, rows_of(part)]
+        return remote(ref, ref, send_s.at[3], p_rs.at[part], sibling)
 
     for part, (first, count) in enumerate(PARTS):
         rows = slice(first, first + count)
 
-        def add_in(i, _, part=part, rows=rows):
-            j = chip_turn(i)
-            red_copy(j, part).wait_recv()
-            own[rows, :] += red_in[j, rows, :].astype(F32)
-            return 0
-
-        lax.fori_loop(0, 7, add_in, 0)
+        all_in = red_in.at[pl.ds(1, 7), rows_of(part)]
+        remote(all_in, all_in, send_s.at[2], b_rs.at[part], sibling).wait_recv()
+        total = own[rows, :]
+        for j in range(1, 8):
+            total = total + red_in[j, rows, :].astype(F32)
         valid = min(first + count, SHARE) - first
         slope = slope_ref[first:first + valid, :].astype(F32)
         curv = curv_ref[first:first + valid, :].astype(F32)
-        weighted = slope * slope * curv * own[first:first + valid, :]
+        weighted = slope * slope * curv * total[:valid]
         if valid < count:
             weighted = jnp.concatenate([weighted, jnp.zeros((count - valid, 128), F32)], axis=0)
         wgt[chan, rows, :] = weighted.astype(BF)
 
         def spread(i, _, part=part):
             j = chip_turn(i)
-            wgt_copy(chan, j, part, chip_dev(j)).start()
+            wgt_copy(chan, part, chip_dev(j)).start()
             return 0
 
         lax.fori_loop(0, 7, spread, 0)
-        wgt_copy(chan, 0, part, sibling).start()
+        sib_wgt_copy(chan, part).start()
 
     lax.fori_loop(4, 8, shift, 0)
 
@@ -335,8 +337,8 @@
         def pass_on(i, _, part=part):
             j = chip_turn(i)
             slot = 2 * chip_at(j, -1) + core
-            wgt_copy(slot, 0, part, sibling).wait_recv()
-            wgt_copy(slot, 7 + j, part, sibling).start()
+            wgt_copy(slot, part, sibling).wait_recv()
+            sib_wgt_copy(slot, part).start()
             unpack(slot, part)
             return 0
 
@@ -346,10 +348,11 @@
     for part in range(2):
 
         def from_sibling(i, _, part=part):
-            slot = 2 * chip_at(chip_turn(lax.rem(i + 7, 8)), -1) + other
-            wgt_copy(slot, 0, part, sibling).wait_recv()
-            unpack(slot, part)
+            unpack(2 * i + other, part)
             return 0
+
+        passed = wgt.at[pl.ds(0, 8), rows_of(part)]
+        remote(passed, passed, send_s.at[3], p_rs.at[part], sibling).wait_recv()
 
         lax.fori_loop(0, 8, from_sibling, 0)
     w32[PIXELS:LANES, :] = jnp.zeros((LANES - PIXELS, 128), F32)
@@ -373,7 +376,7 @@
     scale = F32(1.0) / jnp.sqrt(F32(PIXELS))
 
     def kp_copy(k):
-        return pltpu.make_async_copy(kp_ref.at[k], kp_hbm.at[k], k_s.at[k])
+        return pltpu.make_async_copy(kp_ref.at[k], kp_hbm.at[k], k_s.at[0])
 
     def product(k):
         kp_ref[k] = jnp.dot(xts[k], w16[...], preferred_element_type=F32) * scale
@@ -382,13 +385,13 @@
     def cx_copy(j, part):
         return remote(
             cx_out.at[j, rows_of(part)], cx_in.at[j, rows_of(part)],
-            x_ss.at[2 * j + part], x_rs.at[2 * j + part], across,
+            send_s.at[4], x_rs.at[2 * j + part], across,
         )
 
     def cz_copy(j, part):
         return remote(
             cz_out.at[j, rows_of(part)], cz_in.at[j, rows_of(part)],
-            d_ss.at[2 * j + part], d_rs.at[2 * j + part], z_dev(j),
+            send_s.at[5], d_rs.at[0], z_dev(j),
         )
 
     def to_across(i, _):
@@ -429,38 +432,20 @@
     product(7)
     product(8)
 
-    def add_z(i, _):
-        j = z_turn(i)
-        cz_copy(j, 0).wait_recv()
-        cz_copy(j, 1).wait_recv()
-        own[...] += cz_in[j].astype(F32)
-        return 0
-
-    lax.fori_loop(0, 7, add_z, 0)
-    cot_ref[...] = own[0:SHARE, :].astype(BF)
-
-    for c in sent:
-        c.wait_send()
-    for k in range(TAPS):
-        kp_copy(k).wait()
-
-    def drain(j, _):
-        for part in range(2):
-            sib_copy(j, part).wait_send()
-            cx_copy(j, part).wait_send()
-            wgt_copy(chan, j, part, sibling).wait_send()
-        return 0
-
-    lax.fori_loop(0, 8, drain, 0)
-
-    def drain_far(j, _):
-        for part in range(2):
-            red_copy(j, part).wait_send()
-            cz_copy(j, part).wait_send()
-            wgt_copy(chan, 7 + j, part, sibling).wait_send()
-        return 0
-
-    lax.fori_loop(1, 8, drain_far, 0)
+    others = pl.ds(1, 7)
+    remote(cz_in.at[others], cz_in.at[others], send_s.at[5], d_rs.at[0], across).wait_recv()
+    total = own[...]
+    for j in range(1, 8):
+        total = total + cz_in[j].astype(F32)
+    cot_ref[...] = total[0:SHARE].astype(BF)
+
+    pltpu.make_async_copy(kp_ref, kp_hbm, k_s.at[0]).wait()
+    spent = [
+        gath.at[pl.ds(0, 15)], sib_out, red_out.at[others],
+        wgt.at[pl.ds(0, 15)], cx_out, cz_out.at[others],
+    ]
+    for n, ref in enumerate(spent):
+        remote(ref, ref, send_s.at[n], d_rs.at[0], across).wait_send()
 
 
 def settle(cot_in, kp_in, cot_ref, kp_ref, cot_v, kp_v, in_s, out_s):
@@ -515,10 +500,9 @@
             pltpu.VMEM(share, BF),
             pltpu.VMEM(share, BF),
             pltpu.VMEM(share, BF),
-            dma((6,)), dma((TAPS,)),
-            dma((34,)), dma((16,)), dma((16,)),
-            dma((16,)), dma((16,)), dma((16,)), dma((16,)),
-            dma((32,)), dma((32,)), dma((16,)), dma((16,)), dma((16,)), dma((16,)),
+            dma((6,)), dma((1,)), dma((6,)),
+            dma((16,)), dma((8,)), dma((1,)), dma((16,)), dma((2,)),
+            dma((16,)), dma((2,)), dma((16,)), dma((1,)),
         ],
         compiler_params=pltpu.CompilerParams(
             collective_id=0, has_side_effects=True, vmem_limit_bytes=56 * 1024 * 1024

time: 64.9 us -> 62.9 us (0.969)
  Pallas kernels: 64.1 us -> 62.1 us
    pallas_call x1, Pallas kernels: 62.2 us -> 60.3 us  [per_device(): pl.pallas_call(body, out_shape=shapes, in_specs=[vm] * 2 + [hbm] * 6, out...]
where the time goes in v6:
time: 62.9 us; the launch traced here: 62.8 us
  Pallas kernels  62.1 us (99%)
  between operations  0.64 us (1%)
    pallas_call x1, Pallas kernels, per_device(): pl.pallas_call(body, out_shape=shapes, in_specs=[vm] * 2 + [hbm] * 6, out...  60.3 us
    pallas_call x1, Pallas kernels, per_device(): pl.pallas_call(settle, out_shape=shapes, in_specs=[hbm, hbm], out_specs=(...  1.89 us

profile of v6, /device:TPU:1, one launch (start us, length us, event | category | flops | bytes accessed | tf_op | source)
XLA Modules:
  0.0 62.8 jit_solution(12388742378563570893)
XLA Ops:
  0.6 60.3 %gauss_newton.1 = (bf16[162,128]{1,0:T(8,128)(2,1)}, f32[9,128,128]{2,1,0:T(8,128)}) custom-call(bf16[8,2592]{1,0:T(8,128)(2,1)} %bitcast.2, bf16[8,2592]{1,0:T(8,128)(2,1)} %bitcast.3, bf16[9,128,128]{2,1,0:T(8,128)(2,1)} %w_hbm.1, bf16[9,128,128]{2,1,0:T(8,128)(2,1)} %v_hbm.1, bf16[162,128]{1,0:T(8,128)(2,1)} %slope_hbm.1, bf16[162,128]{1,0:T(8,128)(2,1)} %curv_hbm.1, ...), custom_call_target="tpu_custom_call" | custom-call | tf_op jit(solution)/shard_map/gauss_newton/pallas_call | solution.py:474
  60.9 1.9 %settle.1 = (bf16[162,128]{1,0:T(8,128)(2,1)}, f32[9,128,128]{2,1,0:T(8,128)}) custom-call(bf16[162,128]{1,0:T(8,128)(2,1)} %get-tuple-element.4.cot_in, f32[9,128,128]{2,1,0:T(8,128)} %get-tuple-element.5.kp_in), custom_call_target="tpu_custom_call" | custom-call | tf_op jit(solution)/shard_map/settle/pallas_call | solution.py:515

commit v7 on v6

--- a/solution.py
+++ b/solution.py
@@ -41,9 +41,9 @@
 
 
 def body(
-    acts_ref, tans_ref, w_hbm, v_hbm, slope_hbm, curv_hbm, rmask_hbm, lmask_hbm,
+    acts_hbm, tans_hbm, w_hbm, v_hbm, slope_hbm, curv_hbm, rmask_hbm, lmask_hbm,
     cot_ref, kp_hbm,
-    w_ref, v_ref, slope_ref, curv_ref, rmask, lmask, kp_ref,
+    acts_ref, tans_ref, w_ref, v_ref, slope_ref, curv_ref, rmask, lmask, kp_ref,
     gath, wcat, taps, xts, w32, w16, sib_out, sib_in, red_out, red_in, own,
     wgt, cx_out, cx_in, cz_out, cz_in,
     l_s, k_s,
@@ -97,12 +97,14 @@
         pl.semaphore_signal(barrier, inc=1, device_id=dev, device_id_type=pl.DeviceIdType.MESH)
 
     pairs = [
-        (v_hbm, v_ref), (w_hbm, w_ref), (rmask_hbm, rmask),
+        (acts_hbm, acts_ref), (tans_hbm, tans_ref), (v_hbm, v_ref), (w_hbm, w_ref), (rmask_hbm, rmask),
         (slope_hbm, slope_ref), (curv_hbm, curv_ref), (lmask_hbm, lmask),
     ]
     loads = [pltpu.make_async_copy(src, dst, l_s.at[n]) for n, (src, dst) in enumerate(pairs)]
     for c in loads:
         c.start()
+    for c in loads[:2]:
+        c.wait()
 
     both = jnp.concatenate([acts_ref[...].astype(F32), tans_ref[...].astype(F32)], axis=0)
     both = jnp.concatenate([both, jnp.zeros((16, LANES - PIXELS), F32)], axis=1)
@@ -135,7 +137,7 @@
     send(filt, LOW, right, left, across)
     send(filt, HIGH, across, cross=True)
 
-    for c in loads:
+    for c in loads[2:]:
         c.wait()
     for k in range(TAPS):
         vk = v_ref[k].astype(F32).reshape(16, 1, 8, 128)
@@ -474,9 +476,11 @@
     results = pl.pallas_call(
         body,
         out_shape=shapes,
-        in_specs=[vm] * 2 + [hbm] * 6,
+        in_specs=[hbm] * 8,
         out_specs=(vm, hbm),
         scratch_shapes=[
+            pltpu.VMEM((8, PIXELS), BF),
+            pltpu.VMEM((8, PIXELS), BF),
             pltpu.VMEM((TAPS, 128, 128), BF),
             pltpu.VMEM((TAPS, 128, 128), BF),
             pltpu.VMEM((SHARE, 128), BF),
@@ -500,7 +504,7 @@
             pltpu.VMEM(share, BF),
             pltpu.VMEM(share, BF),
             pltpu.VMEM(share, BF),
-            dma((6,)), dma((1,)), dma((6,)),
+            dma((8,)), dma((1,)), dma((6,)),
             dma((16,)), dma((8,)), dma((1,)), dma((16,)), dma((2,)),
             dma((16,)), dma((2,)), dma((16,)), dma((1,)),
         ],

time: 62.9 us -> 62.3 us (level)
  no operation moved by 1% of the time
where the time goes in v7:
time: 62.3 us; the launch traced here: 62.2 us
  Pallas kernels  61.5 us (99%)
  between operations  0.64 us (1%)
    pallas_call x1, Pallas kernels, per_device(): pl.pallas_call(body, out_shape=shapes, in_specs=[hbm] * 8, out_specs=(vm,...  59.6 us
    pallas_call x1, Pallas kernels, per_device(): pl.pallas_call(settle, out_shape=shapes, in_specs=[hbm, hbm], out_specs=(...  1.89 us

profile of v7, /device:TPU:1, one launch (start us, length us, event | category | flops | bytes accessed | tf_op | source)
XLA Modules:
  0.0 62.2 jit_solution(16448459251883877965)
XLA Ops:
  0.6 59.6 %gauss_newton.1 = (bf16[162,128]{1,0:T(8,128)(2,1)}, f32[9,128,128]{2,1,0:T(8,128)}) custom-call(bf16[8,2592]{1,0:T(8,128)(2,1)} %bitcast.2, bf16[8,2592]{1,0:T(8,128)(2,1)} %bitcast.3, bf16[9,128,128]{2,1,0:T(8,128)(2,1)} %w_hbm.1, bf16[9,128,128]{2,1,0:T(8,128)(2,1)} %v_hbm.1, bf16[162,128]{1,0:T(8,128)(2,1)} %slope_hbm.1, bf16[162,128]{1,0:T(8,128)(2,1)} %curv_hbm.1, ...), custom_call_target="tpu_custom_call" | custom-call | tf_op jit(solution)/shard_map/gauss_newton/pallas_call | solution.py:476
  60.3 1.9 %settle.1 = (bf16[162,128]{1,0:T(8,128)(2,1)}, f32[9,128,128]{2,1,0:T(8,128)}) custom-call(bf16[162,128]{1,0:T(8,128)(2,1)} %get-tuple-element.4.cot_in, f32[9,128,128]{2,1,0:T(8,128)} %get-tuple-element.5.kp_in), custom_call_target="tpu_custom_call" | custom-call | tf_op jit(solution)/shard_map/settle/pallas_call | solution.py:519

commit v8 on v7

--- a/solution.py
+++ b/solution.py
@@ -14,7 +14,7 @@
 CUT = 1152
 SHARE = 162
 ROWS = 176
-PARTS = ((0, 96), (96, 80))
+PARTS = ((0, 80), (80, 96))
 PAD = 16
 BLOCK = 384
 TAPS = 9
@@ -329,10 +329,10 @@
         first, count = PARTS[part]
         x = wgt[c, rows_of(part), :].astype(F32)
         if part == 0:
-            w32[pl.ds(start, 96), :] = x
+            w32[pl.ds(start, count), :] = x
         else:
-            w32[pl.ds(start + 96, 64), :] = x[0:64]
-            w32[pl.ds(start + 160, 2), :] = x[64:66]
+            w32[pl.ds(start + first, 160 - first), :] = x[0:160 - first]
+            w32[pl.ds(start + 160, 2), :] = x[160 - first:162 - first]
 
     for part in range(2):
 
@@ -359,8 +359,14 @@
         lax.fori_loop(0, 8, from_sibling, 0)
     w32[PIXELS:LANES, :] = jnp.zeros((LANES - PIXELS, 128), F32)
 
-    def backward(i, _):
-        t = lax.rem(i + 3 * (1 - half), LANES // BLOCK)
+    def backward(i, _, early=False):
+        base = 3 * (1 - half)
+        if early:
+            start = (theirs + at_z(4)) * SHARE - WW - 1
+            block = lax.div(lax.max(start, 0), BLOCK)
+            t = base + lax.rem(block - base + i, 4)
+        else:
+            t = lax.rem(i + base, LANES // BLOCK)
         rows = pl.ds(pl.multiple_of(t * BLOCK, 16), BLOCK)
         spot = pl.ds(pl.multiple_of(PAD + t * BLOCK, 16), BLOCK)
         w = w32[rows, :].astype(BF)
@@ -373,7 +379,10 @@
                 taps[k + q, spot, :] = res[:, 128 * q:128 * q + 128]
         return 0
 
-    lax.fori_loop(0, 4, backward, 0, unroll=True)
+    def early(i, _):
+        return backward(i, 0, True)
+
+    lax.fori_loop(0, 2, early, 0, unroll=True)
 
     scale = F32(1.0) / jnp.sqrt(F32(PIXELS))
 
@@ -407,7 +416,9 @@
             cx_copy(j, part).start()
         return 0
 
-    lax.fori_loop(0, 8, to_across, 0)
+    to_across(0, 0)
+    lax.fori_loop(2, 4, early, 0, unroll=True)
+    lax.fori_loop(1, 8, to_across, 0)
     lax.fori_loop(4, LANES // BLOCK, backward, 0, unroll=True)
 
     def to_z(i, _):

time: 62.3 us -> 61.5 us (0.987)
  Pallas kernels: 61.5 us -> 60.7 us
    pallas_call x1, Pallas kernels: 59.6 us -> 58.8 us  [per_device(): pl.pallas_call(body, out_shape=shapes, in_specs=[hbm] * 8, out_specs=(vm,...]
where the time goes in v8:
time: 61.5 us; the launch traced here: 61.4 us
  Pallas kernels  60.7 us (99%)
  between operations  0.64 us (1%)
    pallas_call x1, Pallas kernels, per_device(): pl.pallas_call(body, out_shape=shapes, in_specs=[hbm] * 8, out_specs=(vm,...  58.8 us
    pallas_call x1, Pallas kernels, per_device(): pl.pallas_call(settle, out_shape=shapes, in_specs=[hbm, hbm], out_specs=(...  1.89 us

profile of v8, /device:TPU:1, one launch (start us, length us, event | category | flops | bytes accessed | tf_op | source)
XLA Modules:
  0.0 61.4 jit_solution(2383852797630220426)
XLA Ops:
  0.6 58.8 %gauss_newton.1 = (bf16[162,128]{1,0:T(8,128)(2,1)}, f32[9,128,128]{2,1,0:T(8,128)}) custom-call(bf16[8,2592]{1,0:T(8,128)(2,1)} %bitcast.2, bf16[8,2592]{1,0:T(8,128)(2,1)} %bitcast.3, bf16[9,128,128]{2,1,0:T(8,128)(2,1)} %w_hbm.1, bf16[9,128,128]{2,1,0:T(8,128)(2,1)} %v_hbm.1, bf16[162,128]{1,0:T(8,128)(2,1)} %slope_hbm.1, bf16[162,128]{1,0:T(8,128)(2,1)} %curv_hbm.1, ...), custom_call_target="tpu_custom_call" | custom-call | tf_op jit(solution)/shard_map/gauss_newton/pallas_call | solution.py:487
  59.5 1.9 %settle.1 = (bf16[162,128]{1,0:T(8,128)(2,1)}, f32[9,128,128]{2,1,0:T(8,128)}) custom-call(bf16[162,128]{1,0:T(8,128)(2,1)} %get-tuple-element.4.cot_in, f32[9,128,128]{2,1,0:T(8,128)} %get-tuple-element.5.kp_in), custom_call_target="tpu_custom_call" | custom-call | tf_op jit(solution)/shard_map/settle/pallas_call | solution.py:530

commit v9 on v8

--- a/solution.py
+++ b/solution.py
@@ -92,7 +92,7 @@
 
     barrier = pltpu.get_barrier_semaphore()
     peers = [sibling, across, diag_dev(1), diag_dev(-1)]
-    peers += [z_dev(d) for d in range(1, 8)] + [chip_dev(jnp.int32(d)) for d in range(1, 8)]
+    peers += [z_dev(1), z_dev(-1)] + [chip_dev(jnp.int32(d)) for d in range(1, 8)]
     for dev in peers:
         pl.semaphore_signal(barrier, inc=1, device_id=dev, device_id_type=pl.DeviceIdType.MESH)
 

time: 61.5 us -> 61.4 us (level)
  no operation moved by 1% of the time
where the time goes in v9:
time: 61.4 us; the launch traced here: 61.3 us
  Pallas kernels  60.7 us (99%)
  between operations  0.64 us (1%)
    pallas_call x1, Pallas kernels, per_device(): pl.pallas_call(body, out_shape=shapes, in_specs=[hbm] * 8, out_specs=(vm,...  58.8 us
    pallas_call x1, Pallas kernels, per_device(): pl.pallas_call(settle, out_shape=shapes, in_specs=[hbm, hbm], out_specs=(...  1.89 us

profile of v9, /device:TPU:1, one launch (start us, length us, event | category | flops | bytes accessed | tf_op | source)
XLA Modules:
  0.0 61.3 jit_solution(3555376350709429466)
XLA Ops:
  0.6 58.8 %gauss_newton.1 = (bf16[162,128]{1,0:T(8,128)(2,1)}, f32[9,128,128]{2,1,0:T(8,128)}) custom-call(bf16[8,2592]{1,0:T(8,128)(2,1)} %bitcast.2, bf16[8,2592]{1,0:T(8,128)(2,1)} %bitcast.3, bf16[9,128,128]{2,1,0:T(8,128)(2,1)} %w_hbm.1, bf16[9,128,128]{2,1,0:T(8,128)(2,1)} %v_hbm.1, bf16[162,128]{1,0:T(8,128)(2,1)} %slope_hbm.1, bf16[162,128]{1,0:T(8,128)(2,1)} %curv_hbm.1, ...), custom_call_target="tpu_custom_call" | custom-call | tf_op jit(solution)/shard_map/gauss_newton/pallas_call | solution.py:487
  59.4 1.9 %settle.1 = (bf16[162,128]{1,0:T(8,128)(2,1)}, f32[9,128,128]{2,1,0:T(8,128)}) custom-call(bf16[162,128]{1,0:T(8,128)(2,1)} %get-tuple-element.4.cot_in, f32[9,128,128]{2,1,0:T(8,128)} %get-tuple-element.5.kp_in), custom_call_target="tpu_custom_call" | custom-call | tf_op jit(solution)/shard_map/settle/pallas_call | solution.py:530
